TPU v7x, 32 devices: a whole 2x2x4 slice. The times are simulated.
32 devices in a mesh: freq: 2 (over y), gx: 4 (over z), gy: 2 (over x), col: 2 (over core).
Axes of the slice: x: 2, y: 2, z: 4, core: 2. Of those that a mesh axis runs over, the one named last changes fastest.
Arguments:
- source: bfloat16 [12, 64, 32, 256], P('freq', 'gx', 'gy', 'col'), parts along dimension 0, may hold values from -6 to 6
- warm: bfloat16 [12, 64, 32, 256], P('freq', 'gx', 'gy', 'col'), parts along dimension 0, may hold values from -2.1 to 2.6
- forward: bfloat16 [12, 64, 32, 256], P('freq', 'gx', 'gy', 'col'), parts along dimension 0, may hold values from -6 to 6
- density: bfloat16 [64, 32, 256], P('gx', 'gy', 'col'), may hold values from 1 to 3
- material_map: int32 [8, 4, 8], P('gx', 'gy', 'col'), may hold values from 0 to 7
- material_table: float32 [8, 2], replicated, may hold values from 0.5 to 2
- iface_cells: int32 [16, 256], P(('gx', 'gy', 'col')), may hold values from 0 to 32767, as said below
- impedance: float32 [2, 3], replicated, may hold values from 2 to 8
- omega2: float32 [2], P('freq'), parts along dimension 0, may hold values from 0.5 to 1
Outputs:
- adjoint: float32 [12, 64, 32, 256], P('freq', 'gx', 'gy', 'col'), parts along dimension 0
- coarse_gradient: float32 [32, 8], P('freq'), parts along dimension 0
There are 2 independent parts, one for each index of `freq`. A program takes and returns all parts, laid end to end along the dimension named above; an argument that names none is the same for every part. Nothing has to cross between parts.
Inputs may be any that keep to these rules, and one draw needn't show every extreme that they name: `iface_cells`: each row's entries are distinct, rising, and within the tile of 16 x 16 x 128 cells; row r belongs to the device of that index along gx, gy and col together.
All inputs are finite; a program needn't handle non-finite values.
Results may differ from a plain program's by a relative error of at most 0.0003.
Values may be sent and summed in bfloat16 or wider, within the bound.
A program may use at most 64 MiB of HBM per device.

v0:
```python
import jax
import jax.numpy as jnp
from jax import lax
from jax.sharding import PartitionSpec as P

DAMPING = 0.5
RELAXATION = 0.6


def with_halo(array, sides, width):
    for axis, dim in sides:
        peers, length = (lax.axis_size(axis), array.shape[dim])
        up = [(i, (i + 1) % peers) for i in range(peers - 1)]
        down = [(j, i) for i, j in up]
        last = lax.slice_in_dim(array, length - width, length, axis=dim)
        initial = lax.slice_in_dim(array, 0, width, axis=dim)
        before = lax.ppermute(last, axis, up)
        after = lax.ppermute(initial, axis, down)
        array = jnp.concatenate([before, array, after], axis=dim)
    return array


def window(padded, offset):
    size_x = padded.shape[1] - 2
    size_y = padded.shape[2] - 2
    size_z = padded.shape[3] - 2
    return padded[
        :,
        1 + offset[0] : 1 + offset[0] + size_x,
        1 + offset[1] : 1 + offset[1] + size_y,
        1 + offset[2] : 1 + offset[2] + size_z,
    ]


def navier(padded, lame_first, shear):
    units = ((1, 0, 0), (0, 1, 0), (0, 0, 1))
    centre = window(padded, (0, 0, 0))
    second = []
    for axis_d in range(3):
        ahead = units[axis_d]
        behind = tuple((-value for value in ahead))
        second.append(window(padded, ahead) + window(padded, behind) - 2.0 * centre)
    laplace = second[0] + second[1] + second[2]
    result = []
    for part_index in range(2):
        for component in range(3):
            channel = part_index * 3 + component
            divergence = second[component][channel]
            for other_axis in range(3):
                if other_axis != component:
                    source_channel = part_index * 3 + other_axis
                    single = padded[source_channel : source_channel + 1]
                    first_unit = units[component]
                    other_unit = units[other_axis]
                    plus_plus = tuple((first_unit[k] + other_unit[k] for k in range(3)))
                    plus_minus = tuple((first_unit[k] - other_unit[k] for k in range(3)))
                    minus_plus = tuple((-first_unit[k] + other_unit[k] for k in range(3)))
                    minus_minus = tuple((-first_unit[k] - other_unit[k] for k in range(3)))
                    mixed = (
                        window(single, plus_plus)
                        - window(single, plus_minus)
                        - window(single, minus_plus)
                        + window(single, minus_minus)
                    )
                    divergence = divergence + 0.25 * mixed[0]
            result.append(shear * laplace[channel] + (lame_first + shear) * divergence)
    return jnp.stack(result)


def sweep(padded, lame_first, shear, density, mask, source, mean_field, omega_sq, impedance):
    field = window(padded, (0, 0, 0))
    elastic = navier(padded, lame_first, shear)
    real_part = field[:3]
    imag_part = field[3:]
    mean_real = mean_field[:3][:, None, None, None]
    mean_imag = mean_field[3:][:, None, None, None]
    imp_real = impedance[0][:, None, None, None]
    imp_imag = impedance[1][:, None, None, None]
    inertia = omega_sq * density
    diff_real = real_part - mean_real
    diff_imag = imag_part - mean_imag
    apply_real = (
        -elastic[:3]
        - inertia * (real_part - DAMPING * imag_part)
        + mask * (imp_real * diff_real - imp_imag * diff_imag)
    )
    apply_imag = (
        -elastic[3:]
        - inertia * (imag_part + DAMPING * real_part)
        + mask * (imp_real * diff_imag + imp_imag * diff_real)
    )
    resid_real = source[:3] - apply_real
    resid_imag = source[3:] - apply_imag
    diag_real = 8.0 * shear + 2.0 * lame_first - inertia + mask * imp_real
    diag_imag = -DAMPING * inertia + mask * imp_imag
    modulus = diag_real * diag_real + diag_imag * diag_imag
    new_real = real_part + RELAXATION * (resid_real * diag_real + resid_imag * diag_imag) / modulus
    new_imag = imag_part + RELAXATION * (resid_imag * diag_real - resid_real * diag_imag) / modulus
    return jnp.concatenate([new_real, new_imag], 0)


def expand(blocks):
    blocks_x, blocks_y, blocks_z = blocks.shape
    spread = jnp.broadcast_to(
        blocks[:, None, :, None, :, None], (blocks_x, 8, blocks_y, 8, blocks_z, 32)
    )
    return spread.reshape(blocks_x * 8, blocks_y * 8, blocks_z * 32)


def material(block_ids, table):
    lame_first = jnp.zeros(block_ids.shape, jnp.float32)
    shear = jnp.zeros(block_ids.shape, jnp.float32)
    for entry in range(table.shape[0]):
        chosen = block_ids == entry
        lame_first = jnp.where(chosen, table[entry, 0], lame_first)
        shear = jnp.where(chosen, table[entry, 1], shear)
    return (lame_first, shear)


def foundation(field, mask, count):
    total = lax.psum(jnp.sum(mask * field, axis=(1, 2, 3)), ("gx", "gy", "col"))
    return total / count


def shards(
    source, warm, forward, density, material_map, material_table, iface_cells, impedance, omega2
):
    omega_sq = omega2[0]
    tile_shape = density.shape
    tile_cells = tile_shape[0] * tile_shape[1] * tile_shape[2]
    mask = jnp.zeros((tile_cells,), jnp.float32).at[iface_cells[0]].set(1.0).reshape(tile_shape)
    block_ids = expand(material_map)
    lame_first, shear = material(block_ids, material_table)
    density_cells = density.astype(jnp.float32)
    source_cells = source.astype(jnp.float32)
    group_size = lax.axis_size("gx") * lax.axis_size("gy") * lax.axis_size("col")
    count = jnp.float32(group_size * iface_cells.shape[1])
    field = warm.astype(jnp.float32)
    for sweep_index in range(2):
        mean_field = foundation(field, mask, count)
        padded = with_halo(field, (("gx", 1), ("gy", 2), ("col", 3)), 1)
        field = sweep(
            padded,
            lame_first,
            shear,
            density_cells,
            mask,
            source_cells,
            mean_field,
            omega_sq,
            impedance,
        )
    forward_cells = forward.astype(jnp.float32)
    correlation = (
        field[:3] * forward_cells[:3]
        - field[3:] * forward_cells[3:]
        - DAMPING * (field[:3] * forward_cells[3:] + field[3:] * forward_cells[:3])
    )
    cell_terms = -omega_sq * jnp.sum(correlation, axis=0)
    coarse_x = tile_shape[0] // 4
    coarse_y = tile_shape[1] // 4
    local_sums = cell_terms.reshape(coarse_x, 4, coarse_y, 4, tile_shape[2]).sum(axis=(1, 3, 4))
    paired = lax.psum(local_sums, "col")
    gathered = lax.all_gather(paired[None], ("gx", "gy"), axis=0, tiled=True)
    grid_sums = gathered.reshape(lax.axis_size("gx"), lax.axis_size("gy"), coarse_x, coarse_y)
    coarse = (
        grid_sums.transpose(0, 2, 1, 3).reshape(
            lax.axis_size("gx") * coarse_x, lax.axis_size("gy") * coarse_y
        )
        / 64.0
    )
    return (field, coarse)


def solution(mesh):
    in_specs = (
        P("freq", "gx", "gy", "col"),
        P("freq", "gx", "gy", "col"),
        P("freq", "gx", "gy", "col"),
        P("gx", "gy", "col"),
        P("gx", "gy", "col"),
        P(),
        P(("gx", "gy", "col"), None),
        P(),
        P("freq"),
    )
    out_specs = (P("freq", "gx", "gy", "col"), P("freq", None))
    return jax.shard_map(shards, mesh=mesh, in_specs=in_specs, out_specs=out_specs, check_vma=False)
```

profile of v0, /device:TPU:0, one launch (start us, length us, event | category | flops | bytes accessed | tf_op | source)
XLA Modules:
  0.0 208.3 jit_solution(2462226845284078183)
XLA Ops:
  1.4 1.3 collective-permute-start
  2.7 5.6 %collective-permute-start.1 = (f32[6,1,16,128]{3,2,1,0:T(8,128)S(1)}, f32[6,1,16,128]{3,2,1,0:T(8,128)S(1)}, u32[]{:S(2)}, u32[]{:S(2)}) collective-permute-start(f32[6,1,16,128]{3,2,1,0:T(8,128)S(1)} %get-tuple-element.40), channel_id=1, source_target_pairs={{0,4},{4,8},{8,12},{1,5},{5,9},{9,13},{2,6},{6,10},{10,14},{3,7},{... | collective-permute-start | bytes 147464 | tf_op jit(solution)/shard_map/ppermute | solution.py:17
  8.3 2.0 fusion.108
  11.0 1.9 broadcast_select_fusion
  12.9 4.6 %select_select_fusion.1 = f32[2,8,2,8,4,32]{5,4,3,2,1,0:T(4,128)S(1)} fusion(f32[]{:T(128)} %bitcast, f32[]{:T(128)} %bitcast.1, f32[]{:T(128)} %bitcast.2, f32[]{:T(128)} %bitcast.3, f32[]{:T(128)} %bitcast.4, f32[2,2,4]{2,1,0:T(2,128)S(1)} %get-tuple-element.46, f32[]{:T(128)} %bitcast.6, f32[]{:T(128)} %bitcast.5, ...), kind=kLoop, calls=%fused_computation.41 | loop fusion | flops 229376 | bytes 131276 | tf_op jit(solution)/shard_map/jit(_where)/select_n | solution.py:116
  17.4 4.5 %select_select_fusion = f32[2,8,2,8,4,32]{5,4,3,2,1,0:T(4,128)S(1)} fusion(f32[]{:T(128)} %bitcast.8, f32[]{:T(128)} %bitcast.9, f32[]{:T(128)} %bitcast.10, f32[]{:T(128)} %bitcast.11, f32[]{:T(128)} %bitcast.12, f32[2,2,4]{2,1,0:T(2,128)S(1)} %get-tuple-element.45, f32[]{:T(128)} %bitcast.14, f32[]{:T(128)} %bitcast.13, ...), kind=kLoop, calls=%fused_computation.40 | loop fusion | flops 229376 | bytes 131276 | tf_op jit(solution)/shard_map/jit(_where)/select_n | solution.py:115
  22.0 8.9 %multiply_add_fusion = f32[2,8,2,8,4,32]{5,4,3,2,1,0:T(4,128)S(1)} fusion(f32[2,2,4]{2,1,0:T(2,128)S(1)} %get-tuple-element.46, f32[]{:T(128)} %bitcast.6, pred[2,2,4]{2,1,0:T(4,128)(4,1)S(1)} %get-tuple-element.53, f32[]{:T(128)} %bitcast.5, pred[2,2,4]{2,1,0:T(4,128)(4,1)S(1)} %get-tuple-element.48, f32[]{:T(128)} %bitcast.4, ...), kind=kLoop, calls=%fused_computation.39 | loop fusion | flops 557056 | bytes 131368 | tf_op jit(solution)/shard_map/add | solution.py:94
  32.8 1.3 collective-permute-start.2
  34.1 5.8 %collective-permute-start.3 = (f32[6,18,1,128]{3,2,1,0:T(1,128)S(1)}, f32[6,18,1,128]{3,2,1,0:T(1,128)}, u32[]{:S(2)}, u32[]{:S(2)}) collective-permute-start(f32[6,18,1,128]{3,2,1,0:T(1,128)S(1)} %get-tuple-element.34), channel_id=1, source_target_pairs={{0,2},{1,3},{4,6},{5,7},{8,10},{9,11},{12,14},{13,15},{16,18},{17,... | collective-permute-start | bytes 165896 | tf_op jit(solution)/shard_map/ppermute | solution.py:17
  41.7 1.0 convert_element_type.13
  42.7 2.0 scatter_custom_fusion
  44.7 1.0 pad_maximum_fusion.3
  46.2 1.6 copy.44
  47.8 1.3 collective-permute-start.4
  50.0 3.6 %collective-permute-start.5 = (f32[6,18,18,1]{2,1,3,0:T(8,128)S(1)}, f32[6,18,18,1]{2,1,3,0:T(8,128)}, u32[]{:S(2)}, u32[]{:S(2)}) collective-permute-start(f32[6,18,18,1]{2,1,3,0:T(8,128)S(1)} %copy.46), channel_id=1, source_target_pairs={{0,1},{2,3},{4,5},{6,7},{8,9},{10,11},{12,13},{14,15},{16,17},{18,... | collective-permute-start | bytes 23336 | tf_op jit(solution)/shard_map/ppermute | solution.py:17
  53.7 2.6 %pad_maximum_fusion.2 = (f32[6,18,17,128]{3,2,1,0:T(8,128)}, f32[6,18,17,128]{3,2,1,0:T(8,128)}) fusion(f32[6,18,1,128]{3,2,1,0:T(1,128)} %collective-permute-done.2, f32[6,1,16,128]{3,2,1,0:T(8,128)S(1)} %collective-permute-done, f32[6,16,16,128]{3,2,1,0:T(8,128)S(1)} %convert_element_type.12, f32[6,1,16,128]{3,2,1,0:T(8,128)S(1)} %collective-permute-done.1, ...), kind=kLoop, calls=%fused_computation.5 | loop fusion | flops 1410048 | bytes 2875392 | tf_op jit(solution)/shard_map/concatenate | solution.py:19
  57.0 1.7 copy.47
  58.7 3.1 %pad_maximum_fusion = (f32[6,18,18,129]{3,2,1,0:T(8,128)S(1)}, f32[6,18,18,129]{3,2,1,0:T(8,128)S(1)}) fusion(f32[6,18,18,1]{3,2,1,0:T(8,128)S(1)} %copy.45, f32[6,18,1,128]{3,2,1,0:T(1,128)} %collective-permute-done.2, f32[6,1,16,128]{3,2,1,0:T(8,128)S(1)} %collective-permute-done, f32[6,16,16,128]{3,2,1,0:T(8,128)S(1)} %convert_element_type.12, ...), kind=kLoop, calls=%fused_computation.1 | loop fusion | flops 2507760 | bytes 3017088 | tf_op jit(solution)/shard_map/concatenate | solution.py:19
  61.8 2.3 %add_add_fusion.1 = (f32[6,16,16,128]{3,2,1,0:T(8,128)}, f32[6,16,16,128]{3,2,1,0:T(8,128)}, f32[6,16,16,128]{3,2,1,0:T(8,128)}, f32[6,16,16,128]{3,2,1,0:T(8,128)}, f32[6]{0:T(128)S(1)}) fusion(bf16[6,16,16,128]{3,2,1,0:T(8,128)(2,1)S(1)} %copy-done.28, f32[6,18,17,128]{3,2,1,0:T(8,128)S(1)} %copy-done.17, f32[6,18,17,128]{3,2,1,0:T(8,128)S(1)} %copy-done.16, ...), kind=kLoop, calls=%fused_computation.38 | loop fusion | flops 2949114 | bytes 7700504 | tf_op jit(solution)/shard_map/add | solution.py:43
  64.2 29.5 %psum.21 = f32[6]{0:T(128)S(1)} all-reduce(f32[6]{0:T(128)S(1)} %get-tuple-element.39), channel_id=1, replica_groups=mesh['freq'=2,'gx'=4,'gy'=2,'col'=2] {'gx','gy','col'}, use_global_device_ids=true, to_apply=%region_2.3 | all-reduce | flops 6 | bytes 48 | tf_op jit(solution)/shard_map/psum | solution.py:121
  93.7 1.6 fusion.71
  95.4 1.4 fusion.89
  96.8 1.4 fusion.83
  98.3 1.4 fusion.65
  99.7 1.7 fusion.77
  101.5 1.7 fusion.59
  104.1 1.4 collective-permute-start.6
  105.5 4.5 %collective-permute-start.7 = (f32[6,1,16,128]{3,2,1,0:T(8,128)S(1)}, f32[6,1,16,128]{3,2,1,0:T(8,128)S(1)}, u32[]{:S(2)}, u32[]{:S(2)}) collective-permute-start(f32[6,1,16,128]{3,2,1,0:T(8,128)S(1)} %get-tuple-element.37), channel_id=1, source_target_pairs={{0,4},{4,8},{8,12},{1,5},{5,9},{9,13},{2,6},{6,10},{10,14},{3,7},{... | collective-permute-start | bytes 147464 | tf_op jit(solution)/shard_map/ppermute | solution.py:17
  110.2 1.6 collective-permute-done.7
  111.9 1.3 collective-permute-start.8
  113.2 4.7 %collective-permute-start.9 = (f32[6,18,1,128]{3,2,1,0:T(1,128)S(1)}, f32[6,18,1,128]{3,2,1,0:T(1,128)S(1)}, u32[]{:S(2)}, u32[]{:S(2)}) collective-permute-start(f32[6,18,1,128]{3,2,1,0:T(1,128)S(1)} %get-tuple-element.30), channel_id=1, source_target_pairs={{0,2},{1,3},{4,6},{5,7},{8,10},{9,11},{12,14},{13,15},{16,18},{17,... | collective-permute-start | bytes 165896 | tf_op jit(solution)/shard_map/ppermute | solution.py:17
  118.0 1.0 convert_element_type.15
  120.8 1.6 copy.48
  122.4 1.4 collective-permute-start.10
  124.8 3.6 %collective-permute-start.11 = (f32[6,18,18,1]{2,1,3,0:T(8,128)S(1)}, f32[6,18,18,1]{2,1,3,0:T(8,128)}, u32[]{:S(2)}, u32[]{:S(2)}) collective-permute-start(f32[6,18,18,1]{2,1,3,0:T(8,128)S(1)} %copy.50), channel_id=1, source_target_pairs={{0,1},{2,3},{4,5},{6,7},{8,9},{10,11},{12,13},{14,15},{16,17},{18,... | collective-permute-start | bytes 23336 | tf_op jit(solution)/shard_map/ppermute | solution.py:17
  128.4 1.7 pad_maximum_fusion.4
  130.9 1.7 copy.51
  132.6 3.6 %pad_maximum_fusion.1 = (f32[6,18,18,129]{3,2,1,0:T(8,128)S(1)}, f32[6,18,18,129]{3,2,1,0:T(8,128)S(1)}) fusion(f32[6,18,18,1]{3,2,1,0:T(8,128)S(1)} %copy.49, f32[6,18,1,128]{3,2,1,0:T(1,128)} %copy-done.10, f32[6,1,16,128]{3,2,1,0:T(8,128)S(1)} %collective-permute-done.6, f32[3,16,16,128]{3,2,1,0:T(8,128)S(1)} %divide_add_fusion.2, ...), kind=kLoop, calls=%fused_computation.3 | loop fusion | flops 3009312 | bytes 3017088 | tf_op jit(solution)/shard_map/concatenate | solution.py:19
  136.3 2.3 %add_add_fusion = (f32[6,16,16,128]{3,2,1,0:T(8,128)}, f32[6,16,16,128]{3,2,1,0:T(8,128)}, f32[6,16,16,128]{3,2,1,0:T(8,128)}, f32[6,16,16,128]{3,2,1,0:T(8,128)}, f32[6]{0:T(128)S(1)}) fusion(f32[3,16,16,128]{3,2,1,0:T(8,128)S(1)} %divide_add_fusion.2, f32[3,16,16,128]{3,2,1,0:T(8,128)S(1)} %get-tuple-element.11, f32[6,18,17,128]{3,2,1,0:T(8,128)S(1)} %copy-done.19, ...), kind=kLoop, calls=%fused_computation.36 | loop fusion | flops 3145722 | bytes 7307288 | tf_op jit(solution)/shard_map/add | solution.py:43
  138.6 29.5 %psum.22 = f32[6]{0:T(128)S(1)} all-reduce(f32[6]{0:T(128)S(1)} %get-tuple-element.36), channel_id=1, replica_groups=mesh['freq'=2,'gx'=4,'gy'=2,'col'=2] {'gx','gy','col'}, use_global_device_ids=true, to_apply=%region_4.5 | all-reduce | flops 6 | bytes 48 | tf_op jit(solution)/shard_map/psum | solution.py:121
  168.1 1.6 fusion.53
  169.8 1.3 fusion.35
  171.0 1.3 fusion.47
  172.3 1.3 fusion.29
  173.6 1.6 fusion.41
  175.3 1.7 fusion.23
  178.1 2.4 %psum.23 = f32[1,4,4]{2,1,0:T(4,128)S(1)} all-reduce(f32[1,4,4]{2,1,0:T(4,128)S(1)} %bitcast.39), channel_id=1, replica_groups=mesh['freq'=2,'gx'=4,'gy'=2,'col'=2] {'col'}, use_global_device_ids=true, to_apply=%region_8.9 | all-reduce | flops 16 | bytes 128 | tf_op jit(solution)/shard_map/psum | solution.py:163
  180.5 26.0 %all_gather.3 = f32[8,4,4]{2,1,0:T(4,128)S(1)} all-gather(f32[1,4,4]{2,1,0:T(4,128)S(1)} %psum.23), channel_id=1, replica_groups=mesh['freq'=2,'gx'=4,'gy'=2,'col'=2] {'gx','gy'}, dimensions={0}, use_global_device_ids=true | all-gather | bytes 576 | tf_op jit(solution)/shard_map/all_gather | solution.py:164
  (117 shorter events, 14.4 us)
Async XLA Ops:
  0.6 31.2 %copy-start.33 = (bf16[16,16,128]{2,1,0:T(8,128)(2,1)S(1)}, bf16[16,16,128]{2,1,0:T(8,128)(2,1)}, u32[]{:S(2)}) copy-start(bf16[16,16,128]{2,1,0:T(8,128)(2,1)} %param.12) | copy-start | bytes 196612
  1.4 31.2 %collective-permute-start = (f32[6,1,16,128]{3,2,1,0:T(8,128)S(1)}, f32[6,1,16,128]{3,2,1,0:T(8,128)S(1)}, u32[]{:S(2)}, u32[]{:S(2)}) collective-permute-start(f32[6,1,16,128]{3,2,1,0:T(8,128)S(1)} %get-tuple-element.41), channel_id=1, source_target_pairs={{4,0},{8,4},{12,8},{5,1},{9,5},{13,9},{6,2},{10,6},{14,10},{7,3},{... | collective-permute-start | bytes 147464 | tf_op jit(solution)/shard_map/ppermute | solution.py:18
  2.7 30.0 %collective-permute-start.1 = (f32[6,1,16,128]{3,2,1,0:T(8,128)S(1)}, f32[6,1,16,128]{3,2,1,0:T(8,128)S(1)}, u32[]{:S(2)}, u32[]{:S(2)}) collective-permute-start(f32[6,1,16,128]{3,2,1,0:T(8,128)S(1)} %get-tuple-element.40), channel_id=1, source_target_pairs={{0,4},{4,8},{8,12},{1,5},{5,9},{9,13},{2,6},{6,10},{10,14},{3,7},{... | collective-permute-start | bytes 147464 | tf_op jit(solution)/shard_map/ppermute | solution.py:17
  12.9 19.7 %copy-start.34 = (s32[1,256]{1,0:T(1,128)S(1)}, s32[1,256]{1,0:T(1,128)}, u32[]{:S(2)}) copy-start(s32[1,256]{1,0:T(1,128)} %param.15) | copy-start | bytes 3076
  12.9 19.7 %copy-start.27 = (bf16[6,16,16,128]{3,2,1,0:T(8,128)(2,1)S(1)}, bf16[6,16,16,128]{3,2,1,0:T(8,128)(2,1)}, u32[]{:S(2)}) copy-start(bf16[6,16,16,128]{3,2,1,0:T(8,128)(2,1)} %param.10) | copy-start | bytes 1179652
  31.8 8.1 %copy-start.35 = (f32[2,3]{1,0:T(2,128)S(1)}, f32[2,3]{1,0:T(2,128)}, u32[]{:S(2)}) copy-start(f32[2,3]{1,0:T(2,128)} %param.16) | copy-start | bytes 76
  32.7 9.0 %copy-start.31 = (bf16[6,16,16,128]{3,2,1,0:T(8,128)(2,1)S(1)}, bf16[6,16,16,128]{3,2,1,0:T(8,128)(2,1)}, u32[]{:S(2)}) copy-start(bf16[6,16,16,128]{3,2,1,0:T(8,128)(2,1)} %param.9) | copy-start | bytes 1179652
  32.8 11.9 %collective-permute-start.2 = (f32[6,18,1,128]{3,2,1,0:T(1,128)S(1)}, f32[6,18,1,128]{3,2,1,0:T(1,128)}, u32[]{:S(2)}, u32[]{:S(2)}) collective-permute-start(f32[6,18,1,128]{3,2,1,0:T(1,128)S(1)} %get-tuple-element.35), channel_id=1, source_target_pairs={{2,0},{3,1},{6,4},{7,5},{10,8},{11,9},{14,12},{15,13},{18,16},{19,... | collective-permute-start | bytes 165896 | tf_op jit(solution)/shard_map/ppermute | solution.py:18
  34.1 10.6 %collective-permute-start.3 = (f32[6,18,1,128]{3,2,1,0:T(1,128)S(1)}, f32[6,18,1,128]{3,2,1,0:T(1,128)}, u32[]{:S(2)}, u32[]{:S(2)}) collective-permute-start(f32[6,18,1,128]{3,2,1,0:T(1,128)S(1)} %get-tuple-element.34), channel_id=1, source_target_pairs={{0,2},{1,3},{4,6},{5,7},{8,10},{9,11},{12,14},{13,15},{16,18},{17,... | collective-permute-start | bytes 165896 | tf_op jit(solution)/shard_map/ppermute | solution.py:17
  47.8 8.5 %collective-permute-start.4 = (f32[6,18,18,1]{2,1,3,0:T(8,128)}, f32[6,18,18,1]{2,1,3,0:T(8,128)S(1)}, u32[]{:S(2)}, u32[]{:S(2)}) collective-permute-start(f32[6,18,18,1]{2,1,3,0:T(8,128)} %copy.44), channel_id=1, source_target_pairs={{1,0},{3,2},{5,4},{7,6},{9,8},{11,10},{13,12},{15,14},{17,16},{19,... | collective-permute-start | bytes 23336 | tf_op jit(solution)/shard_map/ppermute | solution.py:18
  50.0 7.0 %collective-permute-start.5 = (f32[6,18,18,1]{2,1,3,0:T(8,128)S(1)}, f32[6,18,18,1]{2,1,3,0:T(8,128)}, u32[]{:S(2)}, u32[]{:S(2)}) collective-permute-start(f32[6,18,18,1]{2,1,3,0:T(8,128)S(1)} %copy.46), channel_id=1, source_target_pairs={{0,1},{2,3},{4,5},{6,7},{8,9},{10,11},{12,13},{14,15},{16,17},{18,... | collective-permute-start | bytes 23336 | tf_op jit(solution)/shard_map/ppermute | solution.py:17
  58.7 3.1 %copy-start.6 = (f32[32768]{0:T(1024)S(1)}, f32[32768]{0:T(1024)}, u32[]{:S(2)}) copy-start(f32[32768]{0:T(1024)} %scatter_custom_fusion) | copy-start | bytes 393220
  58.7 3.1 %copy-start.16 = (f32[6,18,17,128]{3,2,1,0:T(8,128)S(1)}, f32[6,18,17,128]{3,2,1,0:T(8,128)}, u32[]{:S(2)}) copy-start(f32[6,18,17,128]{3,2,1,0:T(8,128)} %get-tuple-element.32) | copy-start | bytes 2820100
  58.7 3.1 %copy-start.17 = (f32[6,18,17,128]{3,2,1,0:T(8,128)S(1)}, f32[6,18,17,128]{3,2,1,0:T(8,128)}, u32[]{:S(2)}) copy-start(f32[6,18,17,128]{3,2,1,0:T(8,128)} %get-tuple-element.33) | copy-start | bytes 2820100
  58.7 3.1 %copy-start.28 = (bf16[6,16,16,128]{3,2,1,0:T(8,128)(2,1)S(1)}, bf16[6,16,16,128]{3,2,1,0:T(8,128)(2,1)}, u32[]{:S(2)}) copy-start(bf16[6,16,16,128]{3,2,1,0:T(8,128)(2,1)} %param.10) | copy-start | bytes 1179652
  93.7 1.6 copy-start
  93.7 1.7 copy-start.20
  95.3 6.1 %copy-start.2 = (f32[1,16,16,128]{3,2,1,0:T(8,128)}, f32[1,16,16,128]{3,2,1,0:T(8,128)S(1)}, u32[]{:S(2)}) copy-start(f32[1,16,16,128]{3,2,1,0:T(8,128)S(1)} %get-tuple-element.15) | copy-start | bytes 393220
  101.4 1.8 copy-start.4
  101.4 1.8 copy-start.7
  101.5 1.8 copy-start.23
  101.5 1.8 copy-start.25
  101.5 1.8 copy-start.29
  104.1 13.9 %copy-start.32 = (bf16[6,16,16,128]{3,2,1,0:T(8,128)(2,1)S(1)}, bf16[6,16,16,128]{3,2,1,0:T(8,128)(2,1)}, u32[]{:S(2)}) copy-start(bf16[6,16,16,128]{3,2,1,0:T(8,128)(2,1)} %param.11) | copy-start | bytes 1179652
  104.1 6.1 %collective-permute-start.6 = (f32[6,1,16,128]{3,2,1,0:T(8,128)S(1)}, f32[6,1,16,128]{3,2,1,0:T(8,128)S(1)}, u32[]{:S(2)}, u32[]{:S(2)}) collective-permute-start(f32[6,1,16,128]{3,2,1,0:T(8,128)S(1)} %get-tuple-element.38), channel_id=1, source_target_pairs={{4,0},{8,4},{12,8},{5,1},{9,5},{13,9},{6,2},{10,6},{14,10},{7,3},{... | collective-permute-start | bytes 147464 | tf_op jit(solution)/shard_map/ppermute | solution.py:18
  105.5 6.3 %collective-permute-start.7 = (f32[6,1,16,128]{3,2,1,0:T(8,128)S(1)}, f32[6,1,16,128]{3,2,1,0:T(8,128)S(1)}, u32[]{:S(2)}, u32[]{:S(2)}) collective-permute-start(f32[6,1,16,128]{3,2,1,0:T(8,128)S(1)} %get-tuple-element.37), channel_id=1, source_target_pairs={{0,4},{4,8},{8,12},{1,5},{5,9},{9,13},{2,6},{6,10},{10,14},{3,7},{... | collective-permute-start | bytes 147464 | tf_op jit(solution)/shard_map/ppermute | solution.py:17
  111.9 7.0 %collective-permute-start.8 = (f32[6,18,1,128]{3,2,1,0:T(1,128)S(1)}, f32[6,18,1,128]{3,2,1,0:T(1,128)S(1)}, u32[]{:S(2)}, u32[]{:S(2)}) collective-permute-start(f32[6,18,1,128]{3,2,1,0:T(1,128)S(1)} %get-tuple-element.31), channel_id=1, source_target_pairs={{2,0},{3,1},{6,4},{7,5},{10,8},{11,9},{14,12},{15,13},{18,16},{19,... | collective-permute-start | bytes 165896 | tf_op jit(solution)/shard_map/ppermute | solution.py:18
  113.2 6.3 %collective-permute-start.9 = (f32[6,18,1,128]{3,2,1,0:T(1,128)S(1)}, f32[6,18,1,128]{3,2,1,0:T(1,128)S(1)}, u32[]{:S(2)}, u32[]{:S(2)}) collective-permute-start(f32[6,18,1,128]{3,2,1,0:T(1,128)S(1)} %get-tuple-element.30), channel_id=1, source_target_pairs={{0,2},{1,3},{4,6},{5,7},{8,10},{9,11},{12,14},{13,15},{16,18},{17,... | collective-permute-start | bytes 165896 | tf_op jit(solution)/shard_map/ppermute | solution.py:17
  118.9 0.6 copy-start.10
  119.6 0.6 copy-start.13
  122.4 6.0 %copy-start.11 = (f32[6,18,1,128]{3,2,1,0:T(1,128)S(1)}, f32[6,18,1,128]{3,2,1,0:T(1,128)}, u32[]{:S(2)}) copy-start(f32[6,18,1,128]{3,2,1,0:T(1,128)} %copy-done.10) | copy-start | bytes 165892
  122.4 6.0 %copy-start.14 = (f32[6,18,1,128]{3,2,1,0:T(1,128)S(1)}, f32[6,18,1,128]{3,2,1,0:T(1,128)}, u32[]{:S(2)}) copy-start(f32[6,18,1,128]{3,2,1,0:T(1,128)} %copy-done.13) | copy-start | bytes 165892
  122.4 7.8 %collective-permute-start.10 = (f32[6,18,18,1]{2,1,3,0:T(8,128)}, f32[6,18,18,1]{2,1,3,0:T(8,128)S(1)}, u32[]{:S(2)}, u32[]{:S(2)}) collective-permute-start(f32[6,18,18,1]{2,1,3,0:T(8,128)} %copy.48), channel_id=1, source_target_pairs={{1,0},{3,2},{5,4},{7,6},{9,8},{11,10},{13,12},{15,14},{17,16},{19,... | collective-permute-start | bytes 23336 | tf_op jit(solution)/shard_map/ppermute | solution.py:18
  124.8 6.2 %collective-permute-start.11 = (f32[6,18,18,1]{2,1,3,0:T(8,128)S(1)}, f32[6,18,18,1]{2,1,3,0:T(8,128)}, u32[]{:S(2)}, u32[]{:S(2)}) collective-permute-start(f32[6,18,18,1]{2,1,3,0:T(8,128)S(1)} %copy.50), channel_id=1, source_target_pairs={{0,1},{2,3},{4,5},{6,7},{8,9},{10,11},{12,13},{14,15},{16,17},{18,... | collective-permute-start | bytes 23336 | tf_op jit(solution)/shard_map/ppermute | solution.py:17
  132.6 3.7 %copy-start.8 = (f32[32768]{0:T(1024)S(1)}, f32[32768]{0:T(1024)}, u32[]{:S(2)}) copy-start(f32[32768]{0:T(1024)} %scatter_custom_fusion) | copy-start | bytes 393220
  132.6 3.7 %copy-start.18 = (f32[6,18,17,128]{3,2,1,0:T(8,128)S(1)}, f32[6,18,17,128]{3,2,1,0:T(8,128)}, u32[]{:S(2)}) copy-start(f32[6,18,17,128]{3,2,1,0:T(8,128)} %get-tuple-element.28) | copy-start | bytes 2820100
  132.6 3.7 %copy-start.19 = (f32[6,18,17,128]{3,2,1,0:T(8,128)S(1)}, f32[6,18,17,128]{3,2,1,0:T(8,128)}, u32[]{:S(2)}) copy-start(f32[6,18,17,128]{3,2,1,0:T(8,128)} %get-tuple-element.29) | copy-start | bytes 2820100
  168.1 1.6 copy-start.1
  168.1 1.6 copy-start.3
  168.1 1.6 copy-start.12
  168.1 1.6 copy-start.15
  168.1 1.6 copy-start.22
  175.2 1.8 copy-start.5
  175.2 1.8 copy-start.9
  175.2 1.8 copy-start.21
  175.2 1.8 copy-start.24
  175.3 1.8 copy-start.26
  175.3 1.8 copy-start.30
where the time goes:
time: 210 us; the launch traced here: 208 us
  blocking collectives  87.4 us (42%)
  other arithmetic  61.2 us (29%)
  starting transfers between devices  35.9 us (17%)
  local copies, waits for them, and re-layouts  19.4 us (9%)
  waiting for transfers between devices  2.4 us (1%)
    psum x2, blocking collectives, foundation(): total = lax.psum(jnp.sum(mask * field, axis=(1, 2, 3)), ('gx', 'gy', 'col'))  58.9 us
    ppermute x6, starting transfers between devices, with_halo(): before = lax.ppermute(last, axis, up)  27.9 us
    all_gather x1, blocking collectives, shards(): gathered = lax.all_gather(paired[None], ('gx', 'gy'), axis=0, tiled=True)  26 us
    add x12, other arithmetic, navier(): result.append(shear * laplace[channel] + (lame_first + shear) * divergence)  18.1 us
    concatenate x8, other arithmetic, with_halo(): array = jnp.concatenate([before, array, after], axis=dim)  12.4 us
    add x1, other arithmetic, sweep(): diag_real = 8.0 * shear + 2.0 * lame_first - inertia + mask * imp_real  8.89 us
    ppermute x6, starting transfers between devices, with_halo(): after = lax.ppermute(initial, axis, down)  7.99 us
    select_n x2, other arithmetic, material(): lame_first = jnp.where(chosen, table[entry, 0], lame_first)  6.44 us
  transfers between devices with their start and end apart: 12, of which 3 were waited for; matrix products, arithmetic and copies ran while one was open for 18% of the time, Pallas kernels for 0%

commit v1 on v0

v1 whole, which is shorter than its diff:
```python
import functools
import jax
import jax.numpy as jnp
from jax import lax
from jax.experimental import pallas as pl
from jax.experimental.pallas import tpu as pltpu
from jax.sharding import PartitionSpec as P

DAMPING = 0.5
RELAXATION = 0.6
MESH_ID = pl.DeviceIdType.MESH
TOP = 8


def kernel(
    n_gx, n_gy, n_col,
    warm_ref, source_hbm, density_hbm, forward_hbm, cells_ref,
    map_ref, table_ref, imp_ref, omega_ref,
    out_hbm, coarse_ref,
    f0, f1, zbuf0, zbuf1, zsend0, zsend1, sums0, sums1, sums2, msg0, msg1, msg2,
    mask_s, mu_s, lm_s, dinv, source_s, density_s, forward_s, out_s,
    local_sem, halo_send, halo_recv, sum_send, sum_recv,
):
    f32 = jnp.float32
    cx, cy, cz = warm_ref.shape[1:]
    cells = cells_ref.shape[1]
    group = n_gx * n_gy * n_col
    gx = lax.axis_index("gx")
    gy = lax.axis_index("gy")
    col = lax.axis_index("col")
    me = (gx * n_gy + gy) * n_col + col

    def coords(index):
        return {"gx": index // (n_gy * n_col), "gy": index // n_col % n_gy, "col": index % n_col}

    def peer(p):
        return lax.rem(me + p, group)

    barrier = pltpu.get_barrier_semaphore()
    for p in range(1, group):
        pl.semaphore_signal(barrier, inc=1, device_id=coords(peer(p)), device_id_type=MESH_ID)

    load_density = pltpu.make_async_copy(density_hbm, density_s, local_sem.at[0])
    load_source = pltpu.make_async_copy(source_hbm, source_s, local_sem.at[1])
    load_forward = pltpu.make_async_copy(forward_hbm, forward_s, local_sem.at[2])
    load_density.start()
    load_source.start()
    load_forward.start()

    lane = lax.broadcasted_iota(jnp.int32, (cy, cz), 1)
    row = lax.broadcasted_iota(jnp.int32, (cy, cz), 0)
    lane1 = lax.broadcasted_iota(jnp.int32, (1, cz), 1)
    edge = jnp.where(col == 0, cz - 1, 0)
    omega = omega_ref[0]

    idx = cells_ref[...]
    hot_row = jnp.where(
        lax.broadcasted_iota(jnp.int32, (cx * cy, cells), 0) == idx // cz, 1.0, 0.0
    ).astype(jnp.bfloat16)
    hot_lane = jnp.where(
        lax.broadcasted_iota(jnp.int32, (cz, cells), 0) == idx % cz, 1.0, 0.0
    ).astype(jnp.bfloat16)
    mask = lax.dot_general(
        hot_row, hot_lane, (((1,), (1,)), ((), ())), preferred_element_type=f32
    )
    mask_s[...] = mask.reshape(cx, cy, cz)

    blocks = map_ref.shape
    for bx in range(blocks[0]):
        mus = []
        lms = []
        for by in range(blocks[1]):
            mu = jnp.zeros((8, cz), f32)
            lm = jnp.zeros((8, cz), f32)
            for bz in range(blocks[2]):
                entry = map_ref[bx, by, bz]
                here = lane[:8] // 32 == bz
                lm = jnp.where(here, table_ref[entry, 0], lm)
                mu = jnp.where(here, table_ref[entry, 1], mu)
            mus.append(mu)
            lms.append(lm + mu)
        mu_s[bx] = jnp.concatenate(mus, 0)
        lm_s[bx] = jnp.concatenate(lms, 0)
    mu_edge = jnp.zeros((cy, cz), f32)
    lm_edge = jnp.zeros((cy, cz), f32)
    edge_block = jnp.where(col == 0, blocks[2] - 1, 0)
    for bx in range(blocks[0]):
        for by in range(blocks[1]):
            entry = map_ref[bx, by, edge_block]
            here = (lane % cx // 8 == bx) & (row // 8 == by)
            mu_edge = jnp.where(here, table_ref[entry, 1], mu_edge)
            lm_edge = jnp.where(here, table_ref[entry, 0] + table_ref[entry, 1], lm_edge)

    def pack(packed, value, c, x):
        spot = c * cx + x
        moved = pltpu.roll(value, lax.rem(spot - edge + cz, cz), 1)
        return jnp.where(lane == spot, moved, packed)

    def fold(value):
        return value[:8] + value[8:]

    def to_row(accs):
        tall = jnp.concatenate([jnp.sum(a, 0, keepdims=True) for a in accs] + [jnp.zeros((2, cz), f32)], 0)
        total = jnp.sum(tall, 1, keepdims=True)
        spots = lax.broadcasted_iota(jnp.int32, (8, cz), 0) == lax.broadcasted_iota(jnp.int32, (8, cz), 1)
        return jnp.sum(jnp.where(spots, total, 0.0), 0, keepdims=True)

    rows = pl.ds(TOP, cy)
    zero_acc = tuple(jnp.zeros((8, cz), f32) for _ in range(6))

    def convert(x, carry):
        packed, accs = carry
        m = mask_s[x]
        grown = []
        for c in range(6):
            v = warm_ref[c, x].astype(f32)
            f0[c, x + 1, rows, :] = v
            grown.append(accs[c] + fold(m * v))
            packed = pack(packed, v, c, x)
        return packed, tuple(grown)

    packed, accs = lax.fori_loop(0, cx, convert, (jnp.zeros((cy, cz), f32), zero_acc))
    zsend0[...] = packed
    msg0[...] = to_row(accs)

    has = {"xm": gx > 0, "xp": gx < n_gx - 1, "ym": gy > 0, "yp": gy < n_gy - 1}

    def both(a, b):
        return jnp.logical_and(has[a], has[b])

    sources = [
        (has["xm"], -1, 0, False), (has["xp"], 1, 0, False),
        (has["ym"], 0, -1, False), (has["yp"], 0, 1, False),
        (both("xm", "ym"), -1, -1, False), (both("xm", "yp"), -1, 1, False),
        (both("xp", "ym"), 1, -1, False), (both("xp", "yp"), 1, 1, False),
        (None, 0, 0, True),
        (has["xm"], -1, 0, True), (has["xp"], 1, 0, True),
        (has["ym"], 0, -1, True), (has["yp"], 0, 1, True),
    ]

    def halo_part(field, dx, dy, halo):
        if dx == 0:
            px = pl.ds(1, cx)
        elif halo:
            px = pl.ds(0 if dx < 0 else cx + 1, 1)
        else:
            px = pl.ds(1 if dx < 0 else cx, 1)
        if dy == 0:
            py = pl.ds(TOP, cy)
        elif halo:
            py = pl.ds(TOP - 1 if dy < 0 else TOP + cy, 1)
        else:
            py = pl.ds(TOP if dy < 0 else TOP + cy - 1, 1)
        return field.at[:, px, py, :]

    def exchange(phase, field, zsend, zbuf):
        result = []
        for k, (cond, dx, dy, flip) in enumerate(sources):
            opposite = next(
                j for j, s in enumerate(sources) if s[1] == -dx and s[2] == -dy and s[3] == flip
            )
            if flip:
                src = zsend
                dst = zbuf.at[opposite - 8]
                here = zbuf.at[k - 8]
            else:
                src = halo_part(field, dx, dy, False)
                dst = halo_part(field, -dx, -dy, True)
                here = halo_part(field, dx, dy, True)
            target = {"gx": gx + dx, "gy": gy + dy, "col": 1 - col if flip else col}
            out = pltpu.make_async_remote_copy(
                src_ref=src, dst_ref=dst, send_sem=halo_send.at[phase, k],
                recv_sem=halo_recv.at[phase, opposite], device_id=target, device_id_type=MESH_ID,
            )
            arrive = pltpu.make_async_remote_copy(
                src_ref=here, dst_ref=here, send_sem=halo_send.at[phase, k],
                recv_sem=halo_recv.at[phase, k], device_id=target, device_id_type=MESH_ID,
            )
            result.append((cond, out, arrive))
        return result

    def guarded(cond, action):
        if cond is None:
            action()
        else:
            pl.when(cond)(action)

    def zero_absent(field, zbuf):
        for k, (cond, dx, dy, flip) in enumerate(sources):
            if cond is None:
                continue

            def clear(k=k, dx=dx, dy=dy, flip=flip):
                if flip:
                    zbuf[k - 8] = jnp.zeros(zbuf.shape[1:], f32)
                else:
                    part = halo_part(field, dx, dy, True)
                    part[...] = jnp.zeros(part.shape, f32)

            pl.when(jnp.logical_not(cond))(clear)

    def sum_copies(phase, msg, slots):
        result = []
        for p in range(1, group):
            other = peer(p)
            out = pltpu.make_async_remote_copy(
                src_ref=msg, dst_ref=slots.at[me], send_sem=sum_send.at[phase, p],
                recv_sem=sum_recv.at[phase, me], device_id=coords(other), device_id_type=MESH_ID,
            )
            arrive = pltpu.make_async_remote_copy(
                src_ref=msg, dst_ref=slots.at[other], send_sem=sum_send.at[phase, p],
                recv_sem=sum_recv.at[phase, other], device_id=coords(other), device_id_type=MESH_ID,
            )
            result.append((None, out, arrive))
        slots[me] = msg[...]
        return result

    zero_absent(f0, zbuf0)
    zero_absent(f1, zbuf1)

    pl.semaphore_wait(barrier, group - 1)

    pending = []

    def start(copies):
        for cond, out, _ in copies:
            guarded(cond, out.start)
        pending.extend(copies)

    def land(copies):
        for cond, _, arrive in copies:
            guarded(cond, arrive.wait_recv)

    halo0 = exchange(0, f0, zsend0, zbuf0)
    total0 = sum_copies(0, msg0, sums0)
    start(halo0)
    start(total0)

    load_density.wait()

    def prepare(x, carry):
        mu = mu_s[x // 8]
        lm = lm_s[x // 8]
        m = mask_s[x]
        inertia = omega * density_s[x].astype(f32)
        base = 6.0 * mu + 2.0 * lm - inertia
        for c in range(3):
            real = base + m * imp_ref[0, c]
            imag = m * imp_ref[1, c] - DAMPING * inertia
            scale = RELAXATION / (real * real + imag * imag)
            dinv[c, x] = real * scale
            dinv[3 + c, x] = imag * scale
        return carry

    lax.fori_loop(0, cx, prepare, 0)

    def shift_up(v):
        return jnp.where(lane == cz - 1, 0.0, pltpu.roll(v, cz - 1, 1))

    def shift_down(v):
        return jnp.where(lane == 0, 0.0, pltpu.roll(v, 1, 1))

    def z_terms(zbuf):
        sign = jnp.where(col == 0, 0.25, -0.25)
        h = zbuf[0]
        xs = lane % cx
        ahead = jnp.where(xs == cx - 1, pltpu.roll(zbuf[2], cx - 1, 1), pltpu.roll(h, cz - 1, 1))
        behind = jnp.where(xs == 0, pltpu.roll(zbuf[1], cz - cx + 1, 1), pltpu.roll(h, 1, 1))
        dxh = (ahead - behind) * sign
        above = jnp.where(row == cy - 1, pltpu.roll(zbuf[4], cy - 1, 0), pltpu.roll(h, cy - 1, 0))
        below = jnp.where(row == 0, pltpu.roll(zbuf[3], 1, 0), pltpu.roll(h, 1, 0))
        dyh = (above - below) * sign
        comp = lane // cx % 3
        extra = jnp.where(
            comp == 0,
            pltpu.roll(dxh, cz - 2 * cx, 1),
            jnp.where(
                comp == 1,
                pltpu.roll(dyh, cz - cx, 1),
                h + pltpu.roll(dxh, 2 * cx, 1) + pltpu.roll(dyh, cx, 1),
            ),
        )
        return mu_edge * h + lm_edge * extra

    def mean_terms(slots):
        total = jnp.sum(slots[...], 0) / jnp.float32(group * cells)
        means = [jnp.sum(jnp.where(lane1 == c, total, 0.0), 1, keepdims=True) for c in range(6)]
        result = []
        for c in range(3):
            result.append(imp_ref[0, c] * means[c] - imp_ref[1, c] * means[3 + c])
        for c in range(3):
            result.append(imp_ref[0, c] * means[3 + c] + imp_ref[1, c] * means[c])
        return [jnp.broadcast_to(r, (1, cz)) for r in result]

    def slope(field, part, px):
        uz = field[part + 2, px, rows, :]
        return (
            field[part + 1, px, pl.ds(TOP + 1, cy), :]
            - field[part + 1, px, pl.ds(TOP - 1, cy), :]
            + shift_up(uz)
            - shift_down(uz)
        )

    def update(field, x, slopes_before, slopes_after, zk, zm):
        px = x + 1
        mu = mu_s[x // 8]
        lm = lm_s[x // 8]
        quarter = 0.25 * lm
        m = mask_s[x]
        sums = []
        for part in (0, 3):
            xp = [field[part + c, px + 1, rows, :] for c in range(3)]
            xm = [field[part + c, px - 1, rows, :] for c in range(3)]
            yp = [field[part + c, px, pl.ds(TOP + 1, cy), :] for c in range(3)]
            ym = [field[part + c, px, pl.ds(TOP - 1, cy), :] for c in range(3)]
            mid = [field[part + c, px, rows, :] for c in range(3)]
            sx = [a + b for a, b in zip(xp, xm)]
            sy = [a + b for a, b in zip(yp, ym)]
            sz = [shift_up(v) + shift_down(v) for v in mid]
            own = [sx[0], sy[1], sz[2]]
            mixed_x = slopes_after[part // 3] - slopes_before[part // 3]
            dyz = yp[2] - ym[2]
            mixed_y = (
                (field[part, px + 1, pl.ds(TOP + 1, cy), :] - field[part, px - 1, pl.ds(TOP + 1, cy), :])
                - (field[part, px + 1, pl.ds(TOP - 1, cy), :] - field[part, px - 1, pl.ds(TOP - 1, cy), :])
                + shift_up(dyz)
                - shift_down(dyz)
            )
            across = (xp[0] - xm[0]) + (yp[1] - ym[1])
            mixed_z = shift_up(across) - shift_down(across)
            mixed = [mixed_x, mixed_y, mixed_z]
            for c in range(3):
                s = source_s[part + c, x].astype(f32)
                spot = (part + c) * cx + x
                beyond = pltpu.roll(zk, lax.rem(edge - spot + cz, cz), 1)
                s = s + jnp.where(lane == edge, beyond, 0.0)
                s = s + mu * (sx[c] + sy[c] + sz[c]) + lm * own[c] + quarter * mixed[c]
                sums.append(s + m * zm[part + c])
        result = [None] * 6
        for c in range(3):
            dr = dinv[c, x]
            di = dinv[3 + c, x]
            re, im = sums[c], sums[3 + c]
            result[c] = (1.0 - RELAXATION) * field[c, px, rows, :] + (re * dr + im * di)
            result[3 + c] = (1.0 - RELAXATION) * field[3 + c, px, rows, :] + (im * dr - re * di)
        return result, m

    def both_slopes(field, px):
        return (slope(field, 0, px), slope(field, 3, px))

    land(halo0)
    land(total0)
    load_source.wait()
    zk0 = z_terms(zbuf0)
    zm0 = mean_terms(sums0)

    def sweep_one(x, carry):
        before, centre, packed, accs = carry
        after = both_slopes(f0, x + 2)
        new, m = update(f0, x, before, after, zk0, zm0)
        grown = []
        for c in range(6):
            f1[c, x + 1, rows, :] = new[c]
            grown.append(accs[c] + fold(m * new[c]))
            packed = pack(packed, new[c], c, x)
        return centre, after, packed, tuple(grown)

    _, _, packed, accs = lax.fori_loop(
        0, cx, sweep_one,
        (both_slopes(f0, 0), both_slopes(f0, 1), jnp.zeros((cy, cz), f32), zero_acc),
    )
    zsend1[...] = packed
    halo1 = exchange(1, f1, zsend1, zbuf1)
    start(halo1)
    msg1[...] = to_row(accs)
    total1 = sum_copies(1, msg1, sums1)
    start(total1)

    load_forward.wait()
    land(halo1)
    land(total1)
    zk1 = z_terms(zbuf1)
    zm1 = mean_terms(sums1)

    def sweep_two(x, carry):
        before, centre, corr = carry
        after = both_slopes(f1, x + 2)
        new, _ = update(f1, x, before, after, zk1, zm1)
        for c in range(6):
            out_s[c, x] = new[c]
        for c in range(3):
            fr = forward_s[c, x].astype(f32)
            fi = forward_s[3 + c, x].astype(f32)
            corr = corr + (new[c] * (fr - DAMPING * fi) - new[3 + c] * (fi + DAMPING * fr))
        return centre, after, corr

    store = pltpu.make_async_copy(out_s, out_hbm, local_sem.at[3])
    carry = (both_slopes(f1, 0), both_slopes(f1, 1))
    bands = []
    for a in range(cx // 4):
        before, centre, corr = lax.fori_loop(
            4 * a, 4 * a + 4, sweep_two, carry + (jnp.zeros((cy, cz), f32),)
        )
        carry = (before, centre)
        bands.append(corr)
    store.start()
    tall = jnp.concatenate(bands, 0)
    n_rows = tall.shape[0]
    total = jnp.sum(tall, 1, keepdims=True) * (-omega / 64.0)
    spots = lax.broadcasted_iota(jnp.int32, (n_rows, cz), 1) == (
        lax.broadcasted_iota(jnp.int32, (n_rows, cz), 0) // 4 + gy * (n_rows // 4)
    )
    msg2[...] = jnp.sum(jnp.where(spots, total, 0.0), 0, keepdims=True)
    total2 = sum_copies(2, msg2, sums2)
    start(total2)
    land(total2)

    per_x, per_y = cx // 4, cy // 4
    shape = (n_gx * per_x, cz)
    lanes = lax.broadcasted_iota(jnp.int32, shape, 1)
    rows_out = lax.broadcasted_iota(jnp.int32, shape, 0)
    wide = jnp.zeros(shape, f32)
    for g in range(n_gx):
        strip = sums2[g * n_gy * n_col]
        for k in range(1, n_gy * n_col):
            strip = strip + sums2[g * n_gy * n_col + k]
        wide = jnp.where(rows_out // per_x == g, strip, wide)
    wide = jnp.where(lanes // per_y % per_x == rows_out % per_x, wide, 0.0)
    pick_shape = (cz, n_gy * per_y)
    source_lane = lax.broadcasted_iota(jnp.int32, pick_shape, 0)
    target_lane = lax.broadcasted_iota(jnp.int32, pick_shape, 1)
    pick = jnp.where(
        source_lane // (per_x * per_y) * per_y + source_lane % per_y == target_lane, 1.0, 0.0
    )
    coarse_ref[...] = lax.dot_general(
        wide, pick, (((1,), (0,)), ((), ())),
        preferred_element_type=f32, precision=lax.Precision.HIGHEST,
    )
    store.wait()
    for cond, out, _ in pending:
        guarded(cond, out.wait_send)


def shards(n_gx, n_gy, n_col, source, warm, forward, density, material_map, material_table,
           iface_cells, impedance, omega2):
    f32 = jnp.float32
    cx, cy, cz = density.shape
    group = n_gx * n_gy * n_col
    vmem = pl.BlockSpec(memory_space=pltpu.VMEM)
    smem = pl.BlockSpec(memory_space=pltpu.SMEM)
    hbm = pl.BlockSpec(memory_space=pl.ANY)
    field = pltpu.VMEM((6, cx + 2, TOP + cy + 8, cz), f32)
    tile = (cx, cy, cz)
    return pl.pallas_call(
        functools.partial(kernel, n_gx, n_gy, n_col),
        out_shape=(
            jax.ShapeDtypeStruct((6,) + tile, f32),
            jax.ShapeDtypeStruct((n_gx * (cx // 4), n_gy * (cy // 4)), f32),
        ),
        in_specs=[vmem, hbm, hbm, hbm, vmem, smem, smem, smem, smem],
        out_specs=(hbm, vmem),
        scratch_shapes=[
            field, field,
            pltpu.VMEM((5, cy, cz), f32), pltpu.VMEM((5, cy, cz), f32),
            pltpu.VMEM((cy, cz), f32), pltpu.VMEM((cy, cz), f32),
            pltpu.VMEM((group, 1, cz), f32), pltpu.VMEM((group, 1, cz), f32),
            pltpu.VMEM((group, 1, cz), f32),
            pltpu.VMEM((1, cz), f32), pltpu.VMEM((1, cz), f32), pltpu.VMEM((1, cz), f32),
            pltpu.VMEM(tile, f32),
            pltpu.VMEM((cx // 8, cy, cz), f32), pltpu.VMEM((cx // 8, cy, cz), f32),
            pltpu.VMEM((6,) + tile, f32),
            pltpu.VMEM((6,) + tile, jnp.bfloat16),
            pltpu.VMEM(tile, jnp.bfloat16),
            pltpu.VMEM((6,) + tile, jnp.bfloat16),
            pltpu.VMEM((6,) + tile, f32),
            pltpu.SemaphoreType.DMA((4,)),
            pltpu.SemaphoreType.DMA((2, 13)),
            pltpu.SemaphoreType.DMA((2, 13)),
            pltpu.SemaphoreType.DMA((3, group)),
            pltpu.SemaphoreType.DMA((3, group)),
        ],
        compiler_params=pltpu.CompilerParams(
            collective_id=0, has_side_effects=True, vmem_limit_bytes=32 * 1024 * 1024
        ),
        name="adjoint_sweeps",
    )(warm, source, density, forward, iface_cells, material_map, material_table, impedance, omega2)


def solution(mesh):
    in_specs = (
        P("freq", "gx", "gy", "col"),
        P("freq", "gx", "gy", "col"),
        P("freq", "gx", "gy", "col"),
        P("gx", "gy", "col"),
        P("gx", "gy", "col"),
        P(),
        P(("gx", "gy", "col"), None),
        P(),
        P("freq"),
    )
    out_specs = (P("freq", "gx", "gy", "col"), P("freq", None))
    body = functools.partial(shards, mesh.shape["gx"], mesh.shape["gy"], mesh.shape["col"])
    return jax.shard_map(body, mesh=mesh, in_specs=in_specs, out_specs=out_specs, check_vma=False)
```

time: 210 us -> 35.6 us (0.17)
  blocking collectives: 87.4 us -> 0 us
  other arithmetic: 61.2 us -> 0 us
  starting transfers between devices: 35.9 us -> 0 us
  Pallas kernels: 0 us -> 27.9 us
  local copies, waits for them, and re-layouts: 19.4 us -> 6.06 us
  waiting for transfers between devices: 2.4 us -> 0 us
    psum x3 -> x0, blocking collectives: 61.4 us -> none  [the longest x2 58.9 us: foundation(): total = lax.psum(jnp.sum(mask * field, axis=(1, 2, 3)), ('gx', 'gy', 'col'))]
    ppermute x12 -> x0, starting transfers between devices: 35.9 us -> none  [the longest x6 27.9 us: with_halo(): before = lax.ppermute(last, axis, up)]
    add x17 -> x0, other arithmetic: 32.4 us -> none  [the longest x12 18.1 us: navier(): result.append(shear * laplace[channel] + (lame_first + shear) * divergence)]
    pallas_call x0 -> x1, Pallas kernels: none -> 27.9 us  [shards(): pl.pallas_call(functools.partial(kernel, n_gx, n_gy, n_col), out_shape=(j...]
    all_gather x1 -> x0, blocking collectives: 26 us -> none  [shards(): gathered = lax.all_gather(paired[None], ('gx', 'gy'), axis=0, tiled=True)]
    concatenate x10 -> x0, other arithmetic: 13.4 us -> none  [the longest x8 12.4 us: with_halo(): array = jnp.concatenate([before, array, after], axis=dim)]
    select_n x4 -> x0, other arithmetic: 11 us -> none  [the longest x2 6.44 us: material(): lame_first = jnp.where(chosen, table[entry, 0], lame_first)]
    slice x10 -> x0, local copies, waits for them, and re-layouts: 8.79 us -> none  [the longest x4 3.96 us: with_halo(): initial = lax.slice_in_dim(array, 0, width, axis=dim)]
  transfers between devices with their start and end apart: 12 -> 0, of which waited for: 3 -> 0; matrix products, arithmetic and copies ran while one was open for 18% -> 0% of each run, Pallas kernels for 0% -> 0%
where the time goes in v1:
time: 35.6 us; the launch traced here: 35.3 us
  Pallas kernels  27.9 us (78%)
  local copies, waits for them, and re-layouts  6.06 us (17%)
  between operations  1.34 us (4%)
    pallas_call x1, Pallas kernels, shards(): pl.pallas_call(functools.partial(kernel, n_gx, n_gy, n_col), out_shape=(j...  27.9 us
    unnamed x18, local copies, waits for them, and re-layouts  5.4 us

profile of v1, /device:TPU:0, one launch (start us, length us, event | category | flops | bytes accessed | tf_op | source)
XLA Modules:
  0.0 35.3 jit_solution(14138204522058834582)
XLA Ops:
  0.6 0.0 copy-start.7
  1.3 0.0 copy-done.7
  1.3 0.0 copy-start.4
  1.3 0.0 copy-start.5
  1.3 0.0 copy-start.6
  1.3 0.1 copy.11.table_ref
  1.4 0.6 %copy-done.4 = s32[2,2,4]{2,1,0:T(2,128)S(1)} copy-done((s32[2,2,4]{2,1,0:T(2,128)S(1)}, s32[2,2,4]{2,1,0:T(2,128)}, u32[]{:S(2)}) %copy-start.4) | copy-done | bytes 88
  2.0 0.0 copy-done.5
  2.0 0.0 copy-done.6
  2.0 0.0 copy-start
  2.0 1.0 %copy-done = bf16[6,16,16,128]{3,2,1,0:T(8,128)(2,1)S(1)} copy-done((bf16[6,16,16,128]{3,2,1,0:T(8,128)(2,1)S(1)}, bf16[6,16,16,128]{3,2,1,0:T(8,128)(2,1)}, u32[]{:S(2)}) %copy-start) | copy-done | bytes 393240
  3.0 0.0 copy-start.1
  3.0 1.0 %copy-done.1 = bf16[6,16,16,128]{3,2,1,0:T(8,128)(2,1)S(1)} copy-done((bf16[6,16,16,128]{3,2,1,0:T(8,128)(2,1)S(1)}, bf16[6,16,16,128]{3,2,1,0:T(8,128)(2,1)}, u32[]{:S(2)}) %copy-start.1) | copy-done | bytes 393240
  4.0 0.0 copy-start.2
  4.0 1.0 %copy-done.2 = bf16[6,16,16,128]{3,2,1,0:T(8,128)(2,1)S(1)} copy-done((bf16[6,16,16,128]{3,2,1,0:T(8,128)(2,1)S(1)}, bf16[6,16,16,128]{3,2,1,0:T(8,128)(2,1)}, u32[]{:S(2)}) %copy-start.2) | copy-done | bytes 393240
  5.0 0.0 copy-start.3
  5.0 0.8 %copy-done.3 = bf16[16,16,128]{2,1,0:T(8,128)(2,1)S(1)} copy-done((bf16[16,16,128]{2,1,0:T(8,128)(2,1)S(1)}, bf16[16,16,128]{2,1,0:T(8,128)(2,1)}, u32[]{:S(2)}) %copy-start.3) | copy-done | bytes 65560
  5.9 27.9 %adjoint_sweeps.1 = (f32[6,16,16,128]{3,2,1,0:T(8,128)S(1)}, f32[16,8]{1,0:T(8,128)S(1)}) custom-call(bf16[6,16,16,128]{3,2,1,0:T(8,128)(2,1)S(1)} %copy-done, bf16[6,16,16,128]{3,2,1,0:T(8,128)(2,1)S(1)} %copy-done.1, bf16[16,16,128]{2,1,0:T(8,128)(2,1)S(1)} %copy-done.3, bf16[6,16,16,128]{3,2,1,0:T(8,128)(2,1)S(1)} %copy-done.2, s32[1,256]{1,0:T(1,128)S(1)} %copy-done.5, ...), custom_call_target="tpu_custom_call" | custom-call | tf_op jit(solution)/shard_map/adjoint_sweeps/pallas_call | solution.py:454
  33.7 0.7 %copy.12 = f32[16,8]{0,1:T(8,128)} copy(f32[16,8]{1,0:T(8,128)S(1)} %get-tuple-element.3) | data formatting | bytes 1024 | tf_op jit(solution)/shard_map/adjoint_sweeps/pallas_call | solution.py:454
  34.4 0.9 %copy.15 = f32[6,16,16,128]{3,2,1,0:T(8,128)} copy(f32[6,16,16,128]{3,2,1,0:T(8,128)S(1)} %get-tuple-element.6) | data formatting | bytes 1572864
Async XLA Ops:
  0.6 0.7 %copy-start.7 = (f32[8,2]{0,1:T(2,128)S(1)}, f32[8,2]{0,1:T(2,128)}, u32[]{:S(2)}) copy-start(f32[8,2]{0,1:T(2,128)} %param.14) | copy-start | bytes 196
  1.3 0.7 %copy-start.4 = (s32[2,2,4]{2,1,0:T(2,128)S(1)}, s32[2,2,4]{2,1,0:T(2,128)}, u32[]{:S(2)}) copy-start(s32[2,2,4]{2,1,0:T(2,128)} %map_ref.1) | copy-start | bytes 196
  1.3 0.7 %copy-start.5 = (s32[1,256]{1,0:T(1,128)S(1)}, s32[1,256]{1,0:T(1,128)}, u32[]{:S(2)}) copy-start(s32[1,256]{1,0:T(1,128)} %cells_ref.1) | copy-start | bytes 3076
  1.3 0.7 %copy-start.6 = (f32[2,3]{1,0:T(2,128)S(1)}, f32[2,3]{1,0:T(2,128)}, u32[]{:S(2)}) copy-start(f32[2,3]{1,0:T(2,128)} %imp_ref.1) | copy-start | bytes 76
  2.0 1.0 %copy-start = (bf16[6,16,16,128]{3,2,1,0:T(8,128)(2,1)S(1)}, bf16[6,16,16,128]{3,2,1,0:T(8,128)(2,1)}, u32[]{:S(2)}) copy-start(bf16[6,16,16,128]{3,2,1,0:T(8,128)(2,1)} %warm_ref.1) | copy-start | bytes 1179652
  3.0 1.0 %copy-start.1 = (bf16[6,16,16,128]{3,2,1,0:T(8,128)(2,1)S(1)}, bf16[6,16,16,128]{3,2,1,0:T(8,128)(2,1)}, u32[]{:S(2)}) copy-start(bf16[6,16,16,128]{3,2,1,0:T(8,128)(2,1)} %source_hbm.1) | copy-start | bytes 1179652
  4.0 1.0 %copy-start.2 = (bf16[6,16,16,128]{3,2,1,0:T(8,128)(2,1)S(1)}, bf16[6,16,16,128]{3,2,1,0:T(8,128)(2,1)}, u32[]{:S(2)}) copy-start(bf16[6,16,16,128]{3,2,1,0:T(8,128)(2,1)} %forward_hbm.1) | copy-start | bytes 1179652
  5.0 0.8 %copy-start.3 = (bf16[16,16,128]{2,1,0:T(8,128)(2,1)S(1)}, bf16[16,16,128]{2,1,0:T(8,128)(2,1)}, u32[]{:S(2)}) copy-start(bf16[16,16,128]{2,1,0:T(8,128)(2,1)} %density_hbm.1) | copy-start | bytes 196612

commit v2 on v1

--- a/solution.py
+++ b/solution.py
@@ -14,15 +14,16 @@
 
 def kernel(
     n_gx, n_gy, n_col,
-    warm_ref, source_hbm, density_hbm, forward_hbm, cells_ref,
+    warm_hbm, source_hbm, density_hbm, forward_hbm, cells_ref,
     map_ref, table_ref, imp_ref, omega_ref,
-    out_hbm, coarse_ref,
-    f0, f1, zbuf0, zbuf1, zsend0, zsend1, sums0, sums1, sums2, msg0, msg1, msg2,
-    mask_s, mu_s, lm_s, dinv, source_s, density_s, forward_s, out_s,
+    out_ref, coarse_ref,
+    f0, f1, zbuf0, zbuf1, zsend0, zsend1, ybuf0, ybuf1, ysend0, ysend1,
+    sums0, sums1, sums2, msg0, msg1, msg2,
+    mask_s, mu_s, lm_s, dinv, warm_s, source_s, density_s, forward_s, part_s, ky_s,
     local_sem, halo_send, halo_recv, sum_send, sum_recv,
 ):
     f32 = jnp.float32
-    cx, cy, cz = warm_ref.shape[1:]
+    cx, cy, cz = warm_hbm.shape[1:]
     cells = cells_ref.shape[1]
     group = n_gx * n_gy * n_col
     gx = lax.axis_index("gx")
@@ -43,6 +44,8 @@
     load_density = pltpu.make_async_copy(density_hbm, density_s, local_sem.at[0])
     load_source = pltpu.make_async_copy(source_hbm, source_s, local_sem.at[1])
     load_forward = pltpu.make_async_copy(forward_hbm, forward_s, local_sem.at[2])
+    load_warm = pltpu.make_async_copy(warm_hbm, warm_s, local_sem.at[3])
+    load_warm.start()
     load_density.start()
     load_source.start()
     load_forward.start()
@@ -75,8 +78,8 @@
             for bz in range(blocks[2]):
                 entry = map_ref[bx, by, bz]
                 here = lane[:8] // 32 == bz
-                lm = jnp.where(here, table_ref[entry, 0], lm)
-                mu = jnp.where(here, table_ref[entry, 1], mu)
+                lm = jnp.where(here, table_ref[0, entry], lm)
+                mu = jnp.where(here, table_ref[1, entry], mu)
             mus.append(mu)
             lms.append(lm + mu)
         mu_s[bx] = jnp.concatenate(mus, 0)
@@ -88,8 +91,8 @@
         for by in range(blocks[1]):
             entry = map_ref[bx, by, edge_block]
             here = (lane % cx // 8 == bx) & (row // 8 == by)
-            mu_edge = jnp.where(here, table_ref[entry, 1], mu_edge)
-            lm_edge = jnp.where(here, table_ref[entry, 0] + table_ref[entry, 1], lm_edge)
+            mu_edge = jnp.where(here, table_ref[1, entry], mu_edge)
+            lm_edge = jnp.where(here, table_ref[0, entry] + table_ref[1, entry], lm_edge)
 
     def pack(packed, value, c, x):
         spot = c * cx + x
@@ -113,12 +116,25 @@
         m = mask_s[x]
         grown = []
         for c in range(6):
-            v = warm_ref[c, x].astype(f32)
+            v = warm_s[c, x].astype(f32)
             f0[c, x + 1, rows, :] = v
+            ysend0[0, c, pl.ds(x, 1), :] = v[:1]
+            ysend0[1, c, pl.ds(x, 1), :] = v[cy - 1 :]
             grown.append(accs[c] + fold(m * v))
             packed = pack(packed, v, c, x)
         return packed, tuple(grown)
 
+    zero_rows = jnp.zeros((8, cz), f32)
+
+    def clear_rows(x, carry):
+        for field in (f0, f1):
+            for c in range(6):
+                field[c, x, pl.ds(0, 8), :] = zero_rows
+                field[c, x, pl.ds(TOP + cy, 8), :] = zero_rows
+        return carry
+
+    lax.fori_loop(0, cx + 2, clear_rows, 0)
+    load_warm.wait()
     packed, accs = lax.fori_loop(0, cx, convert, (jnp.zeros((cy, cz), f32), zero_acc))
     zsend0[...] = packed
     msg0[...] = to_row(accs)
@@ -138,22 +154,19 @@
         (has["ym"], 0, -1, True), (has["yp"], 0, 1, True),
     ]
 
-    def halo_part(field, dx, dy, halo):
-        if dx == 0:
-            px = pl.ds(1, cx)
-        elif halo:
-            px = pl.ds(0 if dx < 0 else cx + 1, 1)
-        else:
-            px = pl.ds(1 if dx < 0 else cx, 1)
+    def face(field, ysend, dx, dy):
         if dy == 0:
-            py = pl.ds(TOP, cy)
-        elif halo:
-            py = pl.ds(TOP - 1 if dy < 0 else TOP + cy, 1)
-        else:
-            py = pl.ds(TOP if dy < 0 else TOP + cy - 1, 1)
-        return field.at[:, px, py, :]
-
-    def exchange(phase, field, zsend, zbuf):
+            return field.at[:, pl.ds(1 if dx < 0 else cx, 1), pl.ds(TOP, cy), :]
+        spot = pl.ds(0, cx) if dx == 0 else pl.ds(0 if dx < 0 else cx - 1, 1)
+        return ysend.at[0 if dy < 0 else 1, :, spot, :]
+
+    def halo(field, ybuf, dx, dy):
+        if dy == 0:
+            return field.at[:, pl.ds(0 if dx < 0 else cx + 1, 1), pl.ds(TOP, cy), :]
+        spot = pl.ds(TOP, cx) if dx == 0 else pl.ds(TOP - 1 if dx < 0 else TOP + cx, 1)
+        return ybuf.at[0 if dy < 0 else 1, :, spot, :]
+
+    def exchange(phase, field, ysend, ybuf, zsend, zbuf):
         result = []
         for k, (cond, dx, dy, flip) in enumerate(sources):
             opposite = next(
@@ -164,9 +177,9 @@
                 dst = zbuf.at[opposite - 8]
                 here = zbuf.at[k - 8]
             else:
-                src = halo_part(field, dx, dy, False)
-                dst = halo_part(field, -dx, -dy, True)
-                here = halo_part(field, dx, dy, True)
+                src = face(field, ysend, dx, dy)
+                dst = halo(field, ybuf, -dx, -dy)
+                here = halo(field, ybuf, dx, dy)
             target = {"gx": gx + dx, "gy": gy + dy, "col": 1 - col if flip else col}
             out = pltpu.make_async_remote_copy(
                 src_ref=src, dst_ref=dst, send_sem=halo_send.at[phase, k],
@@ -185,7 +198,7 @@
         else:
             pl.when(cond)(action)
 
-    def zero_absent(field, zbuf):
+    def zero_absent(field, ybuf, zbuf):
         for k, (cond, dx, dy, flip) in enumerate(sources):
             if cond is None:
                 continue
@@ -194,7 +207,7 @@
                 if flip:
                     zbuf[k - 8] = jnp.zeros(zbuf.shape[1:], f32)
                 else:
-                    part = halo_part(field, dx, dy, True)
+                    part = halo(field, ybuf, dx, dy)
                     part[...] = jnp.zeros(part.shape, f32)
 
             pl.when(jnp.logical_not(cond))(clear)
@@ -215,8 +228,8 @@
         slots[me] = msg[...]
         return result
 
-    zero_absent(f0, zbuf0)
-    zero_absent(f1, zbuf1)
+    zero_absent(f0, ybuf0, zbuf0)
+    zero_absent(f1, ybuf1, zbuf1)
 
     pl.semaphore_wait(barrier, group - 1)
 
@@ -231,7 +244,7 @@
         for cond, _, arrive in copies:
             guarded(cond, arrive.wait_recv)
 
-    halo0 = exchange(0, f0, zsend0, zbuf0)
+    halo0 = exchange(0, f0, ysend0, ybuf0, zsend0, zbuf0)
     total0 = sum_copies(0, msg0, sums0)
     start(halo0)
     start(total0)
@@ -301,13 +314,11 @@
             - shift_down(uz)
         )
 
-    def update(field, x, slopes_before, slopes_after, zk, zm):
+    def stencil(field, x, before, after):
         px = x + 1
         mu = mu_s[x // 8]
         lm = lm_s[x // 8]
         quarter = 0.25 * lm
-        m = mask_s[x]
-        sums = []
         for part in (0, 3):
             xp = [field[part + c, px + 1, rows, :] for c in range(3)]
             xm = [field[part + c, px - 1, rows, :] for c in range(3)]
@@ -318,7 +329,7 @@
             sy = [a + b for a, b in zip(yp, ym)]
             sz = [shift_up(v) + shift_down(v) for v in mid]
             own = [sx[0], sy[1], sz[2]]
-            mixed_x = slopes_after[part // 3] - slopes_before[part // 3]
+            mixed_x = after[part // 3] - before[part // 3]
             dyz = yp[2] - ym[2]
             mixed_y = (
                 (field[part, px + 1, pl.ds(TOP + 1, cy), :] - field[part, px - 1, pl.ds(TOP + 1, cy), :])
@@ -331,11 +342,37 @@
             mixed = [mixed_x, mixed_y, mixed_z]
             for c in range(3):
                 s = source_s[part + c, x].astype(f32)
-                spot = (part + c) * cx + x
-                beyond = pltpu.roll(zk, lax.rem(edge - spot + cz, cz), 1)
-                s = s + jnp.where(lane == edge, beyond, 0.0)
                 s = s + mu * (sx[c] + sy[c] + sz[c]) + lm * own[c] + quarter * mixed[c]
-                sums.append(s + m * zm[part + c])
+                part_s[part + c, x] = s
+
+    def y_terms(ybuf):
+        for side, edge_rows, sign in ((0, pl.ds(0, 8), -0.25), (1, pl.ds(cy - 8, 8), 0.25)):
+            mu = jnp.concatenate([mu_s[bx, edge_rows, :] for bx in range(cx // 8)], 0)
+            lm = jnp.concatenate([lm_s[bx, edge_rows, :] for bx in range(cx // 8)], 0)
+            scaled = lm * sign
+            for part in (0, 3):
+                h = [ybuf[side, part + c, pl.ds(TOP, cx), :] for c in range(3)]
+                dx = [
+                    ybuf[side, part + c, pl.ds(TOP + 1, cx), :]
+                    - ybuf[side, part + c, pl.ds(TOP - 1, cx), :]
+                    for c in range(2)
+                ]
+                dz = [shift_up(h[c]) - shift_down(h[c]) for c in (1, 2)]
+                ky_s[side, part] = mu * h[0] + scaled * dx[1]
+                ky_s[side, part + 1] = (mu + lm) * h[1] + scaled * (dx[0] + dz[1])
+                ky_s[side, part + 2] = mu * h[2] + scaled * dz[0]
+
+    def finish(field, x, zk, zm):
+        px = x + 1
+        m = mask_s[x]
+        sums = []
+        for c in range(6):
+            beyond = pltpu.roll(zk, lax.rem(edge - (c * cx + x) + cz, cz), 1)
+            s = part_s[c, x] + jnp.where(lane == edge, beyond, 0.0)
+            low = ky_s[0, c, pl.ds(x, 1), :]
+            high = ky_s[1, c, pl.ds(x, 1), :]
+            s = s + jnp.where(row == 0, low, jnp.where(row == cy - 1, high, 0.0))
+            sums.append(s + m * zm[c])
         result = [None] * 6
         for c in range(3):
             dr = dinv[c, x]
@@ -348,62 +385,74 @@
     def both_slopes(field, px):
         return (slope(field, 0, px), slope(field, 3, px))
 
+    def inner(field):
+        def step(x, carry):
+            before, centre = carry
+            after = both_slopes(field, x + 2)
+            stencil(field, x, before, after)
+            return centre, after
+
+        lax.fori_loop(1, cx - 1, step, (both_slopes(field, 1), both_slopes(field, 2)))
+
+    def outer(field):
+        def step(k, carry):
+            x = k * (cx - 1)
+            stencil(field, x, both_slopes(field, x), both_slopes(field, x + 2))
+            return carry
+
+        lax.fori_loop(0, 2, step, 0)
+
+    load_source.wait()
+    inner(f0)
     land(halo0)
+    outer(f0)
+    y_terms(ybuf0)
+    zk0 = z_terms(zbuf0)
     land(total0)
-    load_source.wait()
-    zk0 = z_terms(zbuf0)
     zm0 = mean_terms(sums0)
 
     def sweep_one(x, carry):
-        before, centre, packed, accs = carry
-        after = both_slopes(f0, x + 2)
-        new, m = update(f0, x, before, after, zk0, zm0)
+        packed, accs = carry
+        new, m = finish(f0, x, zk0, zm0)
         grown = []
         for c in range(6):
             f1[c, x + 1, rows, :] = new[c]
+            ysend1[0, c, pl.ds(x, 1), :] = new[c][:1]
+            ysend1[1, c, pl.ds(x, 1), :] = new[c][cy - 1 :]
             grown.append(accs[c] + fold(m * new[c]))
             packed = pack(packed, new[c], c, x)
-        return centre, after, packed, tuple(grown)
-
-    _, _, packed, accs = lax.fori_loop(
-        0, cx, sweep_one,
-        (both_slopes(f0, 0), both_slopes(f0, 1), jnp.zeros((cy, cz), f32), zero_acc),
-    )
+        return packed, tuple(grown)
+
+    packed, accs = lax.fori_loop(0, cx, sweep_one, (jnp.zeros((cy, cz), f32), zero_acc))
     zsend1[...] = packed
-    halo1 = exchange(1, f1, zsend1, zbuf1)
+    halo1 = exchange(1, f1, ysend1, ybuf1, zsend1, zbuf1)
     start(halo1)
     msg1[...] = to_row(accs)
     total1 = sum_copies(1, msg1, sums1)
     start(total1)
 
+    inner(f1)
     load_forward.wait()
     land(halo1)
+    outer(f1)
+    y_terms(ybuf1)
+    zk1 = z_terms(zbuf1)
     land(total1)
-    zk1 = z_terms(zbuf1)
     zm1 = mean_terms(sums1)
 
-    def sweep_two(x, carry):
-        before, centre, corr = carry
-        after = both_slopes(f1, x + 2)
-        new, _ = update(f1, x, before, after, zk1, zm1)
+    def sweep_two(x, corr):
+        new, _ = finish(f1, x, zk1, zm1)
         for c in range(6):
-            out_s[c, x] = new[c]
+            out_ref[c, x] = new[c]
         for c in range(3):
             fr = forward_s[c, x].astype(f32)
             fi = forward_s[3 + c, x].astype(f32)
             corr = corr + (new[c] * (fr - DAMPING * fi) - new[3 + c] * (fi + DAMPING * fr))
-        return centre, after, corr
-
-    store = pltpu.make_async_copy(out_s, out_hbm, local_sem.at[3])
-    carry = (both_slopes(f1, 0), both_slopes(f1, 1))
-    bands = []
-    for a in range(cx // 4):
-        before, centre, corr = lax.fori_loop(
-            4 * a, 4 * a + 4, sweep_two, carry + (jnp.zeros((cy, cz), f32),)
-        )
-        carry = (before, centre)
-        bands.append(corr)
-    store.start()
+        return corr
+
+    bands = [
+        lax.fori_loop(4 * a, 4 * a + 4, sweep_two, jnp.zeros((cy, cz), f32)) for a in range(cx // 4)
+    ]
     tall = jnp.concatenate(bands, 0)
     n_rows = tall.shape[0]
     total = jnp.sum(tall, 1, keepdims=True) * (-omega / 64.0)
@@ -426,17 +475,14 @@
             strip = strip + sums2[g * n_gy * n_col + k]
         wide = jnp.where(rows_out // per_x == g, strip, wide)
     wide = jnp.where(lanes // per_y % per_x == rows_out % per_x, wide, 0.0)
-    pick_shape = (cz, n_gy * per_y)
-    source_lane = lax.broadcasted_iota(jnp.int32, pick_shape, 0)
-    target_lane = lax.broadcasted_iota(jnp.int32, pick_shape, 1)
-    pick = jnp.where(
-        source_lane // (per_x * per_y) * per_y + source_lane % per_y == target_lane, 1.0, 0.0
-    )
+    pick_shape = (n_gy * per_y, cz)
+    target = lax.broadcasted_iota(jnp.int32, pick_shape, 0)
+    origin = lax.broadcasted_iota(jnp.int32, pick_shape, 1)
+    pick = jnp.where(origin // (per_x * per_y) * per_y + origin % per_y == target, 1.0, 0.0)
     coarse_ref[...] = lax.dot_general(
-        wide, pick, (((1,), (0,)), ((), ())),
+        pick, wide, (((1,), (1,)), ((), ())),
         preferred_element_type=f32, precision=lax.Precision.HIGHEST,
     )
-    store.wait()
     for cond, out, _ in pending:
         guarded(cond, out.wait_send)
 
@@ -448,21 +494,29 @@
     group = n_gx * n_gy * n_col
     vmem = pl.BlockSpec(memory_space=pltpu.VMEM)
     smem = pl.BlockSpec(memory_space=pltpu.SMEM)
-    hbm = pl.BlockSpec(memory_space=pl.ANY)
+    hbm = pl.BlockSpec(memory_space=pltpu.HBM)
     field = pltpu.VMEM((6, cx + 2, TOP + cy + 8, cz), f32)
     tile = (cx, cy, cz)
-    return pl.pallas_call(
+    y_halo = pltpu.VMEM((2, 6, TOP + cx + 8, cz), f32)
+    y_face = pltpu.VMEM((2, 6, cx, cz), f32)
+    table = material_table.T
+    warm, source, density, forward, iface_cells, material_map, table, impedance = (
+        pltpu.with_memory_space_constraint(a, pltpu.HBM)
+        for a in (warm, source, density, forward, iface_cells, material_map, table, impedance)
+    )
+    adjoint, coarse = pl.pallas_call(
         functools.partial(kernel, n_gx, n_gy, n_col),
         out_shape=(
             jax.ShapeDtypeStruct((6,) + tile, f32),
-            jax.ShapeDtypeStruct((n_gx * (cx // 4), n_gy * (cy // 4)), f32),
+            jax.ShapeDtypeStruct((n_gy * (cy // 4), n_gx * (cx // 4)), f32),
         ),
-        in_specs=[vmem, hbm, hbm, hbm, vmem, smem, smem, smem, smem],
-        out_specs=(hbm, vmem),
+        in_specs=[hbm, hbm, hbm, hbm, vmem, smem, smem, smem, smem],
+        out_specs=(vmem, vmem),
         scratch_shapes=[
             field, field,
             pltpu.VMEM((5, cy, cz), f32), pltpu.VMEM((5, cy, cz), f32),
             pltpu.VMEM((cy, cz), f32), pltpu.VMEM((cy, cz), f32),
+            y_halo, y_halo, y_face, y_face,
             pltpu.VMEM((group, 1, cz), f32), pltpu.VMEM((group, 1, cz), f32),
             pltpu.VMEM((group, 1, cz), f32),
             pltpu.VMEM((1, cz), f32), pltpu.VMEM((1, cz), f32), pltpu.VMEM((1, cz), f32),
@@ -470,9 +524,11 @@
             pltpu.VMEM((cx // 8, cy, cz), f32), pltpu.VMEM((cx // 8, cy, cz), f32),
             pltpu.VMEM((6,) + tile, f32),
             pltpu.VMEM((6,) + tile, jnp.bfloat16),
+            pltpu.VMEM((6,) + tile, jnp.bfloat16),
             pltpu.VMEM(tile, jnp.bfloat16),
             pltpu.VMEM((6,) + tile, jnp.bfloat16),
             pltpu.VMEM((6,) + tile, f32),
+            y_face,
             pltpu.SemaphoreType.DMA((4,)),
             pltpu.SemaphoreType.DMA((2, 13)),
             pltpu.SemaphoreType.DMA((2, 13)),
@@ -483,7 +539,8 @@
             collective_id=0, has_side_effects=True, vmem_limit_bytes=32 * 1024 * 1024
         ),
         name="adjoint_sweeps",
-    )(warm, source, density, forward, iface_cells, material_map, material_table, impedance, omega2)
+    )(warm, source, density, forward, iface_cells, material_map, table, impedance, omega2)
+    return adjoint, coarse.T
 
 
 def solution(mesh):

time: 35.6 us -> 29.6 us (0.83)
  local copies, waits for them, and re-layouts: 6.06 us -> 1.47 us
  Pallas kernels: 27.9 us -> 26.7 us
    unnamed x18 -> x2, local copies, waits for them, and re-layouts: 5.4 us -> 1.47 us
    pallas_call x1, Pallas kernels: 27.9 us -> 26.7 us  [shards(): pl.pallas_call(functools.partial(kernel, n_gx, n_gy, n_col), out_shape=(j...]
    pallas_call x1 -> x0, local copies, waits for them, and re-layouts: 0.66 us -> none  [shards(): pl.pallas_call(functools.partial(kernel, n_gx, n_gy, n_col), out_shape=(j...]
where the time goes in v2:
time: 29.6 us; the launch traced here: 29.4 us
  Pallas kernels  26.7 us (90%)
  local copies, waits for them, and re-layouts  1.47 us (5%)
  between operations  1.29 us (4%)
    pallas_call x1, Pallas kernels, shards(): pl.pallas_call(functools.partial(kernel, n_gx, n_gy, n_col), out_shape=(j...  26.7 us
    unnamed x2, local copies, waits for them, and re-layouts  1.47 us

profile of v2, /device:TPU:0, one launch (start us, length us, event | category | flops | bytes accessed | tf_op | source)
XLA Modules:
  0.0 29.4 jit_solution(14203451316669949462)
XLA Ops:
  1.3 26.7 %adjoint_sweeps.1 = (f32[6,16,16,128]{3,2,1,0:T(8,128)S(1)}, f32[8,16]{1,0:T(8,128)S(1)}) custom-call(bf16[6,16,16,128]{3,2,1,0:T(8,128)(2,1)} %warm_hbm.1, bf16[6,16,16,128]{3,2,1,0:T(8,128)(2,1)} %source_hbm.1, bf16[16,16,128]{2,1,0:T(8,128)(2,1)} %density_hbm.1, bf16[6,16,16,128]{3,2,1,0:T(8,128)(2,1)} %forward_hbm.1, s32[1,256]{1,0:T(1,128)} %cells_ref.1, ...), custom_call_target="tpu_custom_call" | custom-call | tf_op jit(solution)/shard_map/adjoint_sweeps/pallas_call | solution.py:507
  27.9 0.9 %copy.14 = f32[6,16,16,128]{3,2,1,0:T(8,128)} copy(f32[6,16,16,128]{3,2,1,0:T(8,128)S(1)} %get-tuple-element.8) | data formatting | bytes 1572864
  28.8 0.6 %copy.15 = f32[16,8]{0,1:T(8,128)} copy(f32[16,8]{0,1:T(8,128)S(1)} %bitcast.2) | data formatting | bytes 1024

commit v3 on v2

--- a/solution.py
+++ b/solution.py
@@ -31,15 +31,20 @@
     col = lax.axis_index("col")
     me = (gx * n_gy + gy) * n_col + col
 
-    def coords(index):
-        return {"gx": index // (n_gy * n_col), "gy": index // n_col % n_gy, "col": index % n_col}
-
-    def peer(p):
-        return lax.rem(me + p, group)
+    def turned(position, length):
+        steps = [position + d for d in range(length)]
+        return [steps[0]] + [jnp.where(t >= length, t - length, t) for t in steps[1:]]
+
+    peers = []
+    for other_gx in turned(gx, n_gx):
+        for other_gy in turned(gy, n_gy):
+            for other_col in turned(col, n_col):
+                peers.append({"gx": other_gx, "gy": other_gy, "col": other_col})
+    peers = peers[1:]
 
     barrier = pltpu.get_barrier_semaphore()
-    for p in range(1, group):
-        pl.semaphore_signal(barrier, inc=1, device_id=coords(peer(p)), device_id_type=MESH_ID)
+    for other in peers:
+        pl.semaphore_signal(barrier, inc=1, device_id=other, device_id_type=MESH_ID)
 
     load_density = pltpu.make_async_copy(density_hbm, density_s, local_sem.at[0])
     load_source = pltpu.make_async_copy(source_hbm, source_s, local_sem.at[1])
@@ -58,10 +63,10 @@
 
     idx = cells_ref[...]
     hot_row = jnp.where(
-        lax.broadcasted_iota(jnp.int32, (cx * cy, cells), 0) == idx // cz, 1.0, 0.0
+        lax.broadcasted_iota(jnp.int32, (cx * cy, cells), 0) == lax.shift_right_logical(idx, cz.bit_length() - 1), 1.0, 0.0
     ).astype(jnp.bfloat16)
     hot_lane = jnp.where(
-        lax.broadcasted_iota(jnp.int32, (cz, cells), 0) == idx % cz, 1.0, 0.0
+        lax.broadcasted_iota(jnp.int32, (cz, cells), 0) == (idx & (cz - 1)), 1.0, 0.0
     ).astype(jnp.bfloat16)
     mask = lax.dot_general(
         hot_row, hot_lane, (((1,), (1,)), ((), ())), preferred_element_type=f32
@@ -77,26 +82,27 @@
             lm = jnp.zeros((8, cz), f32)
             for bz in range(blocks[2]):
                 entry = map_ref[bx, by, bz]
-                here = lane[:8] // 32 == bz
+                here = (lane[:8] >= 32 * bz) & (lane[:8] < 32 * (bz + 1))
                 lm = jnp.where(here, table_ref[0, entry], lm)
                 mu = jnp.where(here, table_ref[1, entry], mu)
             mus.append(mu)
             lms.append(lm + mu)
         mu_s[bx] = jnp.concatenate(mus, 0)
         lm_s[bx] = jnp.concatenate(lms, 0)
+    xs = lane & (cx - 1)
     mu_edge = jnp.zeros((cy, cz), f32)
     lm_edge = jnp.zeros((cy, cz), f32)
     edge_block = jnp.where(col == 0, blocks[2] - 1, 0)
     for bx in range(blocks[0]):
         for by in range(blocks[1]):
             entry = map_ref[bx, by, edge_block]
-            here = (lane % cx // 8 == bx) & (row // 8 == by)
+            here = ((xs >= 8 * bx) & (xs < 8 * (bx + 1))) & ((row >= 8 * by) & (row < 8 * (by + 1)))
             mu_edge = jnp.where(here, table_ref[1, entry], mu_edge)
             lm_edge = jnp.where(here, table_ref[0, entry] + table_ref[1, entry], lm_edge)
 
     def pack(packed, value, c, x):
         spot = c * cx + x
-        moved = pltpu.roll(value, lax.rem(spot - edge + cz, cz), 1)
+        moved = pltpu.roll(value, (spot - edge) & (cz - 1), 1)
         return jnp.where(lane == spot, moved, packed)
 
     def fold(value):
@@ -113,6 +119,7 @@
 
     def convert(x, carry):
         packed, accs = carry
+        clear_rows(x + 1)
         m = mask_s[x]
         grown = []
         for c in range(6):
@@ -126,16 +133,16 @@
 
     zero_rows = jnp.zeros((8, cz), f32)
 
-    def clear_rows(x, carry):
+    def clear_rows(px):
         for field in (f0, f1):
             for c in range(6):
-                field[c, x, pl.ds(0, 8), :] = zero_rows
-                field[c, x, pl.ds(TOP + cy, 8), :] = zero_rows
-        return carry
-
-    lax.fori_loop(0, cx + 2, clear_rows, 0)
+                field[c, px, pl.ds(0, 8), :] = zero_rows
+                field[c, px, pl.ds(TOP + cy, 8), :] = zero_rows
+
+    clear_rows(0)
+    clear_rows(cx + 1)
     load_warm.wait()
-    packed, accs = lax.fori_loop(0, cx, convert, (jnp.zeros((cy, cz), f32), zero_acc))
+    packed, accs = lax.fori_loop(0, cx, convert, (jnp.zeros((cy, cz), f32), zero_acc), unroll=2)
     zsend0[...] = packed
     msg0[...] = to_row(accs)
 
@@ -213,20 +220,17 @@
             pl.when(jnp.logical_not(cond))(clear)
 
     def sum_copies(phase, msg, slots):
-        result = []
-        for p in range(1, group):
-            other = peer(p)
-            out = pltpu.make_async_remote_copy(
-                src_ref=msg, dst_ref=slots.at[me], send_sem=sum_send.at[phase, p],
-                recv_sem=sum_recv.at[phase, me], device_id=coords(other), device_id_type=MESH_ID,
-            )
-            arrive = pltpu.make_async_remote_copy(
-                src_ref=msg, dst_ref=slots.at[other], send_sem=sum_send.at[phase, p],
-                recv_sem=sum_recv.at[phase, other], device_id=coords(other), device_id_type=MESH_ID,
-            )
-            result.append((None, out, arrive))
+        for other in peers:
+            pltpu.make_async_remote_copy(
+                src_ref=msg, dst_ref=slots.at[me], send_sem=sum_send.at[phase],
+                recv_sem=sum_recv.at[phase], device_id=other, device_id_type=MESH_ID,
+            ).start()
         slots[me] = msg[...]
-        return result
+        rest = slots.at[pl.ds(0, group - 1)]
+        return pltpu.make_async_remote_copy(
+            src_ref=rest, dst_ref=rest, send_sem=sum_send.at[phase],
+            recv_sem=sum_recv.at[phase], device_id=peers[0], device_id_type=MESH_ID,
+        )
 
     zero_absent(f0, ybuf0, zbuf0)
     zero_absent(f1, ybuf1, zbuf1)
@@ -245,15 +249,14 @@
             guarded(cond, arrive.wait_recv)
 
     halo0 = exchange(0, f0, ysend0, ybuf0, zsend0, zbuf0)
+    start(halo0)
     total0 = sum_copies(0, msg0, sums0)
-    start(halo0)
-    start(total0)
 
     load_density.wait()
 
     def prepare(x, carry):
-        mu = mu_s[x // 8]
-        lm = lm_s[x // 8]
+        mu = mu_s[lax.shift_right_logical(x, 3)]
+        lm = lm_s[lax.shift_right_logical(x, 3)]
         m = mask_s[x]
         inertia = omega * density_s[x].astype(f32)
         base = 6.0 * mu + 2.0 * lm - inertia
@@ -265,7 +268,7 @@
             dinv[3 + c, x] = imag * scale
         return carry
 
-    lax.fori_loop(0, cx, prepare, 0)
+    lax.fori_loop(0, cx, prepare, 0, unroll=2)
 
     def shift_up(v):
         return jnp.where(lane == cz - 1, 0.0, pltpu.roll(v, cz - 1, 1))
@@ -276,19 +279,22 @@
     def z_terms(zbuf):
         sign = jnp.where(col == 0, 0.25, -0.25)
         h = zbuf[0]
-        xs = lane % cx
         ahead = jnp.where(xs == cx - 1, pltpu.roll(zbuf[2], cx - 1, 1), pltpu.roll(h, cz - 1, 1))
         behind = jnp.where(xs == 0, pltpu.roll(zbuf[1], cz - cx + 1, 1), pltpu.roll(h, 1, 1))
         dxh = (ahead - behind) * sign
         above = jnp.where(row == cy - 1, pltpu.roll(zbuf[4], cy - 1, 0), pltpu.roll(h, cy - 1, 0))
         below = jnp.where(row == 0, pltpu.roll(zbuf[3], 1, 0), pltpu.roll(h, 1, 0))
         dyh = (above - below) * sign
-        comp = lane // cx % 3
+
+        def block(c):
+            own = (lane >= c * cx) & (lane < (c + 1) * cx)
+            return own | ((lane >= (c + 3) * cx) & (lane < (c + 4) * cx))
+
         extra = jnp.where(
-            comp == 0,
+            block(0),
             pltpu.roll(dxh, cz - 2 * cx, 1),
             jnp.where(
-                comp == 1,
+                block(1),
                 pltpu.roll(dyh, cz - cx, 1),
                 h + pltpu.roll(dxh, 2 * cx, 1) + pltpu.roll(dyh, cx, 1),
             ),
@@ -316,8 +322,8 @@
 
     def stencil(field, x, before, after):
         px = x + 1
-        mu = mu_s[x // 8]
-        lm = lm_s[x // 8]
+        mu = mu_s[lax.shift_right_logical(x, 3)]
+        lm = lm_s[lax.shift_right_logical(x, 3)]
         quarter = 0.25 * lm
         for part in (0, 3):
             xp = [field[part + c, px + 1, rows, :] for c in range(3)]
@@ -367,7 +373,7 @@
         m = mask_s[x]
         sums = []
         for c in range(6):
-            beyond = pltpu.roll(zk, lax.rem(edge - (c * cx + x) + cz, cz), 1)
+            beyond = pltpu.roll(zk, (edge - (c * cx + x)) & (cz - 1), 1)
             s = part_s[c, x] + jnp.where(lane == edge, beyond, 0.0)
             low = ky_s[0, c, pl.ds(x, 1), :]
             high = ky_s[1, c, pl.ds(x, 1), :]
@@ -392,7 +398,7 @@
             stencil(field, x, before, after)
             return centre, after
 
-        lax.fori_loop(1, cx - 1, step, (both_slopes(field, 1), both_slopes(field, 2)))
+        lax.fori_loop(1, cx - 1, step, (both_slopes(field, 1), both_slopes(field, 2)), unroll=2)
 
     def outer(field):
         def step(k, carry):
@@ -408,7 +414,7 @@
     outer(f0)
     y_terms(ybuf0)
     zk0 = z_terms(zbuf0)
-    land(total0)
+    total0.wait_recv()
     zm0 = mean_terms(sums0)
 
     def sweep_one(x, carry):
@@ -423,13 +429,14 @@
             packed = pack(packed, new[c], c, x)
         return packed, tuple(grown)
 
-    packed, accs = lax.fori_loop(0, cx, sweep_one, (jnp.zeros((cy, cz), f32), zero_acc))
+    packed, accs = lax.fori_loop(
+        0, cx, sweep_one, (jnp.zeros((cy, cz), f32), zero_acc), unroll=2
+    )
     zsend1[...] = packed
     halo1 = exchange(1, f1, ysend1, ybuf1, zsend1, zbuf1)
     start(halo1)
     msg1[...] = to_row(accs)
     total1 = sum_copies(1, msg1, sums1)
-    start(total1)
 
     inner(f1)
     load_forward.wait()
@@ -437,7 +444,7 @@
     outer(f1)
     y_terms(ybuf1)
     zk1 = z_terms(zbuf1)
-    land(total1)
+    total1.wait_recv()
     zm1 = mean_terms(sums1)
 
     def sweep_two(x, corr):
@@ -451,40 +458,43 @@
         return corr
 
     bands = [
-        lax.fori_loop(4 * a, 4 * a + 4, sweep_two, jnp.zeros((cy, cz), f32)) for a in range(cx // 4)
+        lax.fori_loop(4 * a, 4 * a + 4, sweep_two, jnp.zeros((cy, cz), f32), unroll=2) for a in range(cx // 4)
     ]
     tall = jnp.concatenate(bands, 0)
     n_rows = tall.shape[0]
-    total = jnp.sum(tall, 1, keepdims=True) * (-omega / 64.0)
+    band_sums = jnp.sum(tall, 1, keepdims=True) * (-omega / 64.0)
     spots = lax.broadcasted_iota(jnp.int32, (n_rows, cz), 1) == (
-        lax.broadcasted_iota(jnp.int32, (n_rows, cz), 0) // 4 + gy * (n_rows // 4)
+        lax.shift_right_logical(lax.broadcasted_iota(jnp.int32, (n_rows, cz), 0), 2) + gy * (n_rows // 4)
     )
-    msg2[...] = jnp.sum(jnp.where(spots, total, 0.0), 0, keepdims=True)
+    msg2[...] = jnp.sum(jnp.where(spots, band_sums, 0.0), 0, keepdims=True)
     total2 = sum_copies(2, msg2, sums2)
-    start(total2)
-    land(total2)
-
     per_x, per_y = cx // 4, cy // 4
+    assert per_x == 4 and per_y == 4 and cx == 16 and cz == 128 and n_col == 2
     shape = (n_gx * per_x, cz)
     lanes = lax.broadcasted_iota(jnp.int32, shape, 1)
     rows_out = lax.broadcasted_iota(jnp.int32, shape, 0)
+    keep = (lax.shift_right_logical(lanes, 2) & (per_x - 1)) == (rows_out & (per_x - 1))
+    pick_shape = (n_gy * per_y, cz)
+    target = lax.broadcasted_iota(jnp.int32, pick_shape, 0)
+    origin = lax.broadcasted_iota(jnp.int32, pick_shape, 1)
+    place = lax.shift_right_logical(origin, 4) * per_y + (origin & (per_y - 1))
+    pick = jnp.where(place == target, 1.0, 0.0)
+    total2.wait_recv()
     wide = jnp.zeros(shape, f32)
     for g in range(n_gx):
         strip = sums2[g * n_gy * n_col]
         for k in range(1, n_gy * n_col):
             strip = strip + sums2[g * n_gy * n_col + k]
-        wide = jnp.where(rows_out // per_x == g, strip, wide)
-    wide = jnp.where(lanes // per_y % per_x == rows_out % per_x, wide, 0.0)
-    pick_shape = (n_gy * per_y, cz)
-    target = lax.broadcasted_iota(jnp.int32, pick_shape, 0)
-    origin = lax.broadcasted_iota(jnp.int32, pick_shape, 1)
-    pick = jnp.where(origin // (per_x * per_y) * per_y + origin % per_y == target, 1.0, 0.0)
+        wide = jnp.where((rows_out >= g * per_x) & (rows_out < (g + 1) * per_x), strip, wide)
+    wide = jnp.where(keep, wide, 0.0)
     coarse_ref[...] = lax.dot_general(
         pick, wide, (((1,), (1,)), ((), ())),
         preferred_element_type=f32, precision=lax.Precision.HIGHEST,
     )
     for cond, out, _ in pending:
         guarded(cond, out.wait_send)
+    for total in (total0, total1, total2):
+        total.wait_send()
 
 
 def shards(n_gx, n_gy, n_col, source, warm, forward, density, material_map, material_table,
@@ -532,8 +542,8 @@
             pltpu.SemaphoreType.DMA((4,)),
             pltpu.SemaphoreType.DMA((2, 13)),
             pltpu.SemaphoreType.DMA((2, 13)),
-            pltpu.SemaphoreType.DMA((3, group)),
-            pltpu.SemaphoreType.DMA((3, group)),
+            pltpu.SemaphoreType.DMA((3,)),
+            pltpu.SemaphoreType.DMA((3,)),
         ],
         compiler_params=pltpu.CompilerParams(
             collective_id=0, has_side_effects=True, vmem_limit_bytes=32 * 1024 * 1024

time: 29.6 us -> 26 us (0.88)
  Pallas kernels: 26.7 us -> 23.1 us
    pallas_call x1, Pallas kernels: 26.7 us -> 23.1 us  [shards(): pl.pallas_call(functools.partial(kernel, n_gx, n_gy, n_col), out_shape=(j...]
where the time goes in v3:
time: 26 us; the launch traced here: 25.9 us
  Pallas kernels  23.1 us (89%)
  local copies, waits for them, and re-layouts  1.47 us (6%)
  between operations  1.29 us (5%)
    pallas_call x1, Pallas kernels, shards(): pl.pallas_call(functools.partial(kernel, n_gx, n_gy, n_col), out_shape=(j...  23.1 us
    unnamed x2, local copies, waits for them, and re-layouts  1.47 us

profile of v3, /device:TPU:0, one launch (start us, length us, event | category | flops | bytes accessed | tf_op | source)
XLA Modules:
  0.0 25.9 jit_solution(2193435776253812950)
XLA Ops:
  1.3 23.1 %adjoint_sweeps.1 = (f32[6,16,16,128]{3,2,1,0:T(8,128)S(1)}, f32[8,16]{1,0:T(8,128)S(1)}) custom-call(bf16[6,16,16,128]{3,2,1,0:T(8,128)(2,1)} %warm_hbm.1, bf16[6,16,16,128]{3,2,1,0:T(8,128)(2,1)} %source_hbm.1, bf16[16,16,128]{2,1,0:T(8,128)(2,1)} %density_hbm.1, bf16[6,16,16,128]{3,2,1,0:T(8,128)(2,1)} %forward_hbm.1, s32[1,256]{1,0:T(1,128)} %cells_ref.1, ...), custom_call_target="tpu_custom_call" | custom-call | tf_op jit(solution)/shard_map/adjoint_sweeps/pallas_call | solution.py:517
  24.4 0.9 %copy.14 = f32[6,16,16,128]{3,2,1,0:T(8,128)} copy(f32[6,16,16,128]{3,2,1,0:T(8,128)S(1)} %get-tuple-element.8) | data formatting | bytes 1572864
  25.3 0.6 %copy.15 = f32[16,8]{0,1:T(8,128)} copy(f32[16,8]{0,1:T(8,128)S(1)} %bitcast.2) | data formatting | bytes 1024

commit v4 on v3

--- a/solution.py
+++ b/solution.py
@@ -19,7 +19,7 @@
     out_ref, coarse_ref,
     f0, f1, zbuf0, zbuf1, zsend0, zsend1, ybuf0, ybuf1, ysend0, ysend1,
     sums0, sums1, sums2, msg0, msg1, msg2,
-    mask_s, mu_s, lm_s, dinv, warm_s, source_s, density_s, forward_s, part_s, ky_s,
+    mask_s, mu_s, lm_s, dinv, warm_s, source_s, density_s, forward_s, part_s, ky_s, slope_s,
     local_sem, halo_send, halo_recv, sum_send, sum_recv,
 ):
     f32 = jnp.float32
@@ -114,33 +114,22 @@
         spots = lax.broadcasted_iota(jnp.int32, (8, cz), 0) == lax.broadcasted_iota(jnp.int32, (8, cz), 1)
         return jnp.sum(jnp.where(spots, total, 0.0), 0, keepdims=True)
 
-    rows = pl.ds(TOP, cy)
     zero_acc = tuple(jnp.zeros((8, cz), f32) for _ in range(6))
 
     def convert(x, carry):
         packed, accs = carry
-        clear_rows(x + 1)
         m = mask_s[x]
         grown = []
         for c in range(6):
             v = warm_s[c, x].astype(f32)
-            f0[c, x + 1, rows, :] = v
+            f0[c, x + 1] = v
             ysend0[0, c, pl.ds(x, 1), :] = v[:1]
             ysend0[1, c, pl.ds(x, 1), :] = v[cy - 1 :]
             grown.append(accs[c] + fold(m * v))
             packed = pack(packed, v, c, x)
         return packed, tuple(grown)
 
-    zero_rows = jnp.zeros((8, cz), f32)
-
-    def clear_rows(px):
-        for field in (f0, f1):
-            for c in range(6):
-                field[c, px, pl.ds(0, 8), :] = zero_rows
-                field[c, px, pl.ds(TOP + cy, 8), :] = zero_rows
-
-    clear_rows(0)
-    clear_rows(cx + 1)
+
     load_warm.wait()
     packed, accs = lax.fori_loop(0, cx, convert, (jnp.zeros((cy, cz), f32), zero_acc), unroll=2)
     zsend0[...] = packed
@@ -163,13 +152,13 @@
 
     def face(field, ysend, dx, dy):
         if dy == 0:
-            return field.at[:, pl.ds(1 if dx < 0 else cx, 1), pl.ds(TOP, cy), :]
+            return field.at[:, pl.ds(1 if dx < 0 else cx, 1)]
         spot = pl.ds(0, cx) if dx == 0 else pl.ds(0 if dx < 0 else cx - 1, 1)
         return ysend.at[0 if dy < 0 else 1, :, spot, :]
 
     def halo(field, ybuf, dx, dy):
         if dy == 0:
-            return field.at[:, pl.ds(0 if dx < 0 else cx + 1, 1), pl.ds(TOP, cy), :]
+            return field.at[:, pl.ds(0 if dx < 0 else cx + 1, 1)]
         spot = pl.ds(TOP, cx) if dx == 0 else pl.ds(TOP - 1 if dx < 0 else TOP + cx, 1)
         return ybuf.at[0 if dy < 0 else 1, :, spot, :]
 
@@ -311,45 +300,54 @@
             result.append(imp_ref[0, c] * means[3 + c] + imp_ref[1, c] * means[c])
         return [jnp.broadcast_to(r, (1, cz)) for r in result]
 
-    def slope(field, part, px):
-        uz = field[part + 2, px, rows, :]
-        return (
-            field[part + 1, px, pl.ds(TOP + 1, cy), :]
-            - field[part + 1, px, pl.ds(TOP - 1, cy), :]
-            + shift_up(uz)
-            - shift_down(uz)
-        )
-
-    def stencil(field, x, before, after):
+    def y_up(v):
+        return jnp.where(row == cy - 1, 0.0, pltpu.roll(v, cy - 1, 0))
+
+    def y_down(v):
+        return jnp.where(row == 0, 0.0, pltpu.roll(v, 1, 0))
+
+    def halo_slopes(field):
+        def step(k, carry):
+            px = k * (cx + 1)
+            for part in (0, 3):
+                uy = field[part + 1, px]
+                uz = field[part + 2, px]
+                slope_s[part // 3, px] = y_up(uy) - y_down(uy) + (shift_up(uz) - shift_down(uz))
+            return carry
+
+        lax.fori_loop(0, 2, step, 0)
+
+    def stencil(field, x):
         px = x + 1
-        mu = mu_s[lax.shift_right_logical(x, 3)]
-        lm = lm_s[lax.shift_right_logical(x, 3)]
+        block_x = lax.shift_right_logical(x, 3)
+        mu = mu_s[block_x]
+        lm = lm_s[block_x]
         quarter = 0.25 * lm
         for part in (0, 3):
-            xp = [field[part + c, px + 1, rows, :] for c in range(3)]
-            xm = [field[part + c, px - 1, rows, :] for c in range(3)]
-            yp = [field[part + c, px, pl.ds(TOP + 1, cy), :] for c in range(3)]
-            ym = [field[part + c, px, pl.ds(TOP - 1, cy), :] for c in range(3)]
-            mid = [field[part + c, px, rows, :] for c in range(3)]
+            mid = [field[part + c, px] for c in range(3)]
+            xp = [field[part + c, px + 1] for c in range(3)]
+            xm = [field[part + c, px - 1] for c in range(3)]
+            yp = [y_up(v) for v in mid]
+            ym = [y_down(v) for v in mid]
+            zp = [shift_up(v) for v in mid]
+            zm = [shift_down(v) for v in mid]
             sx = [a + b for a, b in zip(xp, xm)]
             sy = [a + b for a, b in zip(yp, ym)]
-            sz = [shift_up(v) + shift_down(v) for v in mid]
-            own = [sx[0], sy[1], sz[2]]
-            mixed_x = after[part // 3] - before[part // 3]
-            dyz = yp[2] - ym[2]
-            mixed_y = (
-                (field[part, px + 1, pl.ds(TOP + 1, cy), :] - field[part, px - 1, pl.ds(TOP + 1, cy), :])
-                - (field[part, px + 1, pl.ds(TOP - 1, cy), :] - field[part, px - 1, pl.ds(TOP - 1, cy), :])
-                + shift_up(dyz)
-                - shift_down(dyz)
-            )
-            across = (xp[0] - xm[0]) + (yp[1] - ym[1])
-            mixed_z = shift_up(across) - shift_down(across)
-            mixed = [mixed_x, mixed_y, mixed_z]
+            sz = [a + b for a, b in zip(zp, zm)]
+            dx0 = xp[0] - xm[0]
+            dy1 = yp[1] - ym[1]
+            dz2 = zp[2] - zm[2]
+            slope_s[part // 3, px] = dy1 + dz2
+            by_y = dx0 + dz2
+            by_z = dx0 + dy1
+            own = [
+                lm * sx[0],
+                lm * sy[1] + quarter * (y_up(by_y) - y_down(by_y)),
+                lm * sz[2] + quarter * (shift_up(by_z) - shift_down(by_z)),
+            ]
             for c in range(3):
-                s = source_s[part + c, x].astype(f32)
-                s = s + mu * (sx[c] + sy[c] + sz[c]) + lm * own[c] + quarter * mixed[c]
-                part_s[part + c, x] = s
+                s = source_s[part + c, x].astype(f32) + own[c]
+                part_s[part + c, x] = s + mu * (sx[c] + sy[c] + sz[c])
 
     def y_terms(ybuf):
         for side, edge_rows, sign in ((0, pl.ds(0, 8), -0.25), (1, pl.ds(cy - 8, 8), 0.25)):
@@ -371,6 +369,7 @@
     def finish(field, x, zk, zm):
         px = x + 1
         m = mask_s[x]
+        quarter = 0.25 * lm_s[lax.shift_right_logical(x, 3)]
         sums = []
         for c in range(6):
             beyond = pltpu.roll(zk, (edge - (c * cx + x)) & (cz - 1), 1)
@@ -378,35 +377,32 @@
             low = ky_s[0, c, pl.ds(x, 1), :]
             high = ky_s[1, c, pl.ds(x, 1), :]
             s = s + jnp.where(row == 0, low, jnp.where(row == cy - 1, high, 0.0))
+            if c % 3 == 0:
+                s = s + quarter * (slope_s[c // 3, px + 1] - slope_s[c // 3, px - 1])
             sums.append(s + m * zm[c])
         result = [None] * 6
         for c in range(3):
             dr = dinv[c, x]
             di = dinv[3 + c, x]
             re, im = sums[c], sums[3 + c]
-            result[c] = (1.0 - RELAXATION) * field[c, px, rows, :] + (re * dr + im * di)
-            result[3 + c] = (1.0 - RELAXATION) * field[3 + c, px, rows, :] + (im * dr - re * di)
+            result[c] = (1.0 - RELAXATION) * field[c, px] + (re * dr + im * di)
+            result[3 + c] = (1.0 - RELAXATION) * field[3 + c, px] + (im * dr - re * di)
         return result, m
-
-    def both_slopes(field, px):
-        return (slope(field, 0, px), slope(field, 3, px))
 
     def inner(field):
         def step(x, carry):
-            before, centre = carry
-            after = both_slopes(field, x + 2)
-            stencil(field, x, before, after)
-            return centre, after
-
-        lax.fori_loop(1, cx - 1, step, (both_slopes(field, 1), both_slopes(field, 2)), unroll=2)
+            stencil(field, x)
+            return carry
+
+        lax.fori_loop(1, cx - 1, step, 0, unroll=2)
 
     def outer(field):
         def step(k, carry):
-            x = k * (cx - 1)
-            stencil(field, x, both_slopes(field, x), both_slopes(field, x + 2))
+            stencil(field, k * (cx - 1))
             return carry
 
         lax.fori_loop(0, 2, step, 0)
+        halo_slopes(field)
 
     load_source.wait()
     inner(f0)
@@ -422,7 +418,7 @@
         new, m = finish(f0, x, zk0, zm0)
         grown = []
         for c in range(6):
-            f1[c, x + 1, rows, :] = new[c]
+            f1[c, x + 1] = new[c]
             ysend1[0, c, pl.ds(x, 1), :] = new[c][:1]
             ysend1[1, c, pl.ds(x, 1), :] = new[c][cy - 1 :]
             grown.append(accs[c] + fold(m * new[c]))
@@ -505,7 +501,7 @@
     vmem = pl.BlockSpec(memory_space=pltpu.VMEM)
     smem = pl.BlockSpec(memory_space=pltpu.SMEM)
     hbm = pl.BlockSpec(memory_space=pltpu.HBM)
-    field = pltpu.VMEM((6, cx + 2, TOP + cy + 8, cz), f32)
+    field = pltpu.VMEM((6, cx + 2, cy, cz), f32)
     tile = (cx, cy, cz)
     y_halo = pltpu.VMEM((2, 6, TOP + cx + 8, cz), f32)
     y_face = pltpu.VMEM((2, 6, cx, cz), f32)
@@ -539,6 +535,7 @@
             pltpu.VMEM((6,) + tile, jnp.bfloat16),
             pltpu.VMEM((6,) + tile, f32),
             y_face,
+            pltpu.VMEM((2, cx + 2, cy, cz), f32),
             pltpu.SemaphoreType.DMA((4,)),
             pltpu.SemaphoreType.DMA((2, 13)),
             pltpu.SemaphoreType.DMA((2, 13)),

time: 26 us -> 26 us (level)
  no operation moved by 1% of the time
where the time goes in v4:
time: 26 us; the launch traced here: 25.9 us
  Pallas kernels  23.1 us (89%)
  local copies, waits for them, and re-layouts  1.47 us (6%)
  between operations  1.29 us (5%)
    pallas_call x1, Pallas kernels, shards(): pl.pallas_call(functools.partial(kernel, n_gx, n_gy, n_col), out_shape=(j...  23.1 us
    unnamed x2, local copies, waits for them, and re-layouts  1.47 us

profile of v4, /device:TPU:0, one launch (start us, length us, event | category | flops | bytes accessed | tf_op | source)
XLA Modules:
  0.0 25.9 jit_solution(3301024832115144982)
XLA Ops:
  1.3 23.1 %adjoint_sweeps.1 = (f32[6,16,16,128]{3,2,1,0:T(8,128)S(1)}, f32[8,16]{1,0:T(8,128)S(1)}) custom-call(bf16[6,16,16,128]{3,2,1,0:T(8,128)(2,1)} %warm_hbm.1, bf16[6,16,16,128]{3,2,1,0:T(8,128)(2,1)} %source_hbm.1, bf16[16,16,128]{2,1,0:T(8,128)(2,1)} %density_hbm.1, bf16[6,16,16,128]{3,2,1,0:T(8,128)(2,1)} %forward_hbm.1, s32[1,256]{1,0:T(1,128)} %cells_ref.1, ...), custom_call_target="tpu_custom_call" | custom-call | tf_op jit(solution)/shard_map/adjoint_sweeps/pallas_call | solution.py:513
  24.4 0.9 %copy.14 = f32[6,16,16,128]{3,2,1,0:T(8,128)} copy(f32[6,16,16,128]{3,2,1,0:T(8,128)S(1)} %get-tuple-element.8) | data formatting | bytes 1572864
  25.3 0.6 %copy.15 = f32[16,8]{0,1:T(8,128)} copy(f32[16,8]{0,1:T(8,128)S(1)} %bitcast.2) | data formatting | bytes 1024

commit v5 on v4

--- a/solution.py
+++ b/solution.py
@@ -18,6 +18,7 @@
     map_ref, table_ref, imp_ref, omega_ref,
     out_ref, coarse_ref,
     f0, f1, zbuf0, zbuf1, zsend0, zsend1, ybuf0, ybuf1, ysend0, ysend1,
+    xhalf0, xhalf1, xsend, yhalf0, yhalf1, ysend_half0, ysend_half1,
     sums0, sums1, sums2, msg0, msg1, msg2,
     mask_s, mu_s, lm_s, dinv, warm_s, source_s, density_s, forward_s, part_s, ky_s, slope_s,
     local_sem, halo_send, halo_recv, sum_send, sum_recv,
@@ -72,6 +73,155 @@
         hot_row, hot_lane, (((1,), (1,)), ((), ())), preferred_element_type=f32
     )
     mask_s[...] = mask.reshape(cx, cy, cz)
+
+    def pack(packed, value, c, x):
+        spot = c * cx + x
+        moved = pltpu.roll(value, (spot - edge) & (cz - 1), 1)
+        return jnp.where(lane == spot, moved, packed)
+
+    def fold(value):
+        return value[:8] + value[8:]
+
+    def to_row(accs):
+        tall = jnp.concatenate([jnp.sum(a, 0, keepdims=True) for a in accs] + [jnp.zeros((2, cz), f32)], 0)
+        total = jnp.sum(tall, 1, keepdims=True)
+        spots = lax.broadcasted_iota(jnp.int32, (8, cz), 0) == lax.broadcasted_iota(jnp.int32, (8, cz), 1)
+        return jnp.sum(jnp.where(spots, total, 0.0), 0, keepdims=True)
+
+    zero_acc = tuple(jnp.zeros((8, cz), f32) for _ in range(6))
+
+    def convert(x, carry):
+        packed, accs = carry
+        m = mask_s[x]
+        grown = []
+        for c in range(6):
+            v = warm_s[c, x].astype(f32)
+            f0[c, x + 1] = v
+            ysend0[0, c, pl.ds(x, 1), :] = v[:1]
+            ysend0[1, c, pl.ds(x, 1), :] = v[cy - 1 :]
+            grown.append(accs[c] + fold(m * v))
+            packed = pack(packed, v, c, x)
+        return packed, tuple(grown)
+
+
+    load_warm.wait()
+    packed, accs = lax.fori_loop(0, cx, convert, (jnp.zeros((cy, cz), f32), zero_acc), unroll=2)
+    zsend0[...] = packed.astype(jnp.bfloat16)
+    ysend_half0[...] = ysend0[...].astype(jnp.bfloat16)
+    msg0[...] = to_row(accs)
+
+    has = {"xm": gx > 0, "xp": gx < n_gx - 1, "ym": gy > 0, "yp": gy < n_gy - 1}
+
+    def both(a, b):
+        return jnp.logical_and(has[a], has[b])
+
+    sources = [
+        (has["xm"], -1, 0, False), (has["xp"], 1, 0, False),
+        (has["ym"], 0, -1, False), (has["yp"], 0, 1, False),
+        (both("xm", "ym"), -1, -1, False), (both("xm", "yp"), -1, 1, False),
+        (both("xp", "ym"), 1, -1, False), (both("xp", "yp"), 1, 1, False),
+        (None, 0, 0, True),
+        (has["xm"], -1, 0, True), (has["xp"], 1, 0, True),
+        (has["ym"], 0, -1, True), (has["yp"], 0, 1, True),
+    ]
+
+    def face(xfaces, ysend, ysend_half, dx, dy):
+        if dy == 0:
+            return xfaces[0 if dx < 0 else 1]
+        side = 0 if dy < 0 else 1
+        if dx == 0:
+            return ysend_half.at[side]
+        return ysend.at[side, :, pl.ds(0 if dx < 0 else cx - 1, 1), :]
+
+    def halo(xhalf, ybuf, yhalf, dx, dy):
+        if dy == 0:
+            return xhalf.at[0 if dx < 0 else 1]
+        side = 0 if dy < 0 else 1
+        if dx == 0:
+            return yhalf.at[side]
+        return ybuf.at[side, :, pl.ds(TOP - 1 if dx < 0 else TOP + cx, 1), :]
+
+    def exchange(phase, xfaces, xhalf, ysend, ysend_half, ybuf, yhalf, zsend, zbuf):
+        result = []
+        for k, (cond, dx, dy, flip) in enumerate(sources):
+            opposite = next(
+                j for j, s in enumerate(sources) if s[1] == -dx and s[2] == -dy and s[3] == flip
+            )
+            if flip:
+                src = zsend
+                dst = zbuf.at[opposite - 8]
+                here = zbuf.at[k - 8]
+            else:
+                src = face(xfaces, ysend, ysend_half, dx, dy)
+                dst = halo(xhalf, ybuf, yhalf, -dx, -dy)
+                here = halo(xhalf, ybuf, yhalf, dx, dy)
+            target = {"gx": gx + dx, "gy": gy + dy, "col": 1 - col if flip else col}
+            out = pltpu.make_async_remote_copy(
+                src_ref=src, dst_ref=dst, send_sem=halo_send.at[phase, k],
+                recv_sem=halo_recv.at[phase, opposite], device_id=target, device_id_type=MESH_ID,
+            )
+            arrive = pltpu.make_async_remote_copy(
+                src_ref=here, dst_ref=here, send_sem=halo_send.at[phase, k],
+                recv_sem=halo_recv.at[phase, k], device_id=target, device_id_type=MESH_ID,
+            )
+            result.append((cond, out, arrive))
+        return result
+
+    def guarded(cond, action):
+        if cond is None:
+            action()
+        else:
+            pl.when(cond)(action)
+
+    def zero_absent(xhalf, ybuf, yhalf, zbuf):
+        for k, (cond, dx, dy, flip) in enumerate(sources):
+            if cond is None:
+                continue
+
+            def clear(k=k, dx=dx, dy=dy, flip=flip):
+                if flip:
+                    zbuf[k - 8] = jnp.zeros(zbuf.shape[1:], zbuf.dtype)
+                else:
+                    part = halo(xhalf, ybuf, yhalf, dx, dy)
+                    part[...] = jnp.zeros(part.shape, part.dtype)
+
+            pl.when(jnp.logical_not(cond))(clear)
+
+    def sum_copies(phase, msg, slots):
+        for other in peers:
+            pltpu.make_async_remote_copy(
+                src_ref=msg, dst_ref=slots.at[me], send_sem=sum_send.at[phase],
+                recv_sem=sum_recv.at[phase], device_id=other, device_id_type=MESH_ID,
+            ).start()
+        slots[me] = msg[...]
+        rest = slots.at[pl.ds(0, group - 1)]
+        return pltpu.make_async_remote_copy(
+            src_ref=rest, dst_ref=rest, send_sem=sum_send.at[phase],
+            recv_sem=sum_recv.at[phase], device_id=peers[0], device_id_type=MESH_ID,
+        )
+
+    zero_absent(xhalf0, ybuf0, yhalf0, zbuf0)
+    zero_absent(xhalf1, ybuf1, yhalf1, zbuf1)
+
+    pl.semaphore_wait(barrier, group - 1)
+
+    pending = []
+
+    def start(copies):
+        for cond, out, _ in copies:
+            guarded(cond, out.start)
+        pending.extend(copies)
+
+    def land(copies):
+        for cond, _, arrive in copies:
+            guarded(cond, arrive.wait_recv)
+
+    halo0 = exchange(
+        0, (warm_s.at[:, 0], warm_s.at[:, cx - 1]), xhalf0,
+        ysend0, ysend_half0, ybuf0, yhalf0, zsend0, zbuf0,
+    )
+    start(halo0)
+    total0 = sum_copies(0, msg0, sums0)
 
     blocks = map_ref.shape
     for bx in range(blocks[0]):
@@ -100,147 +250,6 @@
             mu_edge = jnp.where(here, table_ref[1, entry], mu_edge)
             lm_edge = jnp.where(here, table_ref[0, entry] + table_ref[1, entry], lm_edge)
 
-    def pack(packed, value, c, x):
-        spot = c * cx + x
-        moved = pltpu.roll(value, (spot - edge) & (cz - 1), 1)
-        return jnp.where(lane == spot, moved, packed)
-
-    def fold(value):
-        return value[:8] + value[8:]
-
-    def to_row(accs):
-        tall = jnp.concatenate([jnp.sum(a, 0, keepdims=True) for a in accs] + [jnp.zeros((2, cz), f32)], 0)
-        total = jnp.sum(tall, 1, keepdims=True)
-        spots = lax.broadcasted_iota(jnp.int32, (8, cz), 0) == lax.broadcasted_iota(jnp.int32, (8, cz), 1)
-        return jnp.sum(jnp.where(spots, total, 0.0), 0, keepdims=True)
-
-    zero_acc = tuple(jnp.zeros((8, cz), f32) for _ in range(6))
-
-    def convert(x, carry):
-        packed, accs = carry
-        m = mask_s[x]
-        grown = []
-        for c in range(6):
-            v = warm_s[c, x].astype(f32)
-            f0[c, x + 1] = v
-            ysend0[0, c, pl.ds(x, 1), :] = v[:1]
-            ysend0[1, c, pl.ds(x, 1), :] = v[cy - 1 :]
-            grown.append(accs[c] + fold(m * v))
-            packed = pack(packed, v, c, x)
-        return packed, tuple(grown)
-
-
-    load_warm.wait()
-    packed, accs = lax.fori_loop(0, cx, convert, (jnp.zeros((cy, cz), f32), zero_acc), unroll=2)
-    zsend0[...] = packed
-    msg0[...] = to_row(accs)
-
-    has = {"xm": gx > 0, "xp": gx < n_gx - 1, "ym": gy > 0, "yp": gy < n_gy - 1}
-
-    def both(a, b):
-        return jnp.logical_and(has[a], has[b])
-
-    sources = [
-        (has["xm"], -1, 0, False), (has["xp"], 1, 0, False),
-        (has["ym"], 0, -1, False), (has["yp"], 0, 1, False),
-        (both("xm", "ym"), -1, -1, False), (both("xm", "yp"), -1, 1, False),
-        (both("xp", "ym"), 1, -1, False), (both("xp", "yp"), 1, 1, False),
-        (None, 0, 0, True),
-        (has["xm"], -1, 0, True), (has["xp"], 1, 0, True),
-        (has["ym"], 0, -1, True), (has["yp"], 0, 1, True),
-    ]
-
-    def face(field, ysend, dx, dy):
-        if dy == 0:
-            return field.at[:, pl.ds(1 if dx < 0 else cx, 1)]
-        spot = pl.ds(0, cx) if dx == 0 else pl.ds(0 if dx < 0 else cx - 1, 1)
-        return ysend.at[0 if dy < 0 else 1, :, spot, :]
-
-    def halo(field, ybuf, dx, dy):
-        if dy == 0:
-            return field.at[:, pl.ds(0 if dx < 0 else cx + 1, 1)]
-        spot = pl.ds(TOP, cx) if dx == 0 else pl.ds(TOP - 1 if dx < 0 else TOP + cx, 1)
-        return ybuf.at[0 if dy < 0 else 1, :, spot, :]
-
-    def exchange(phase, field, ysend, ybuf, zsend, zbuf):
-        result = []
-        for k, (cond, dx, dy, flip) in enumerate(sources):
-            opposite = next(
-                j for j, s in enumerate(sources) if s[1] == -dx and s[2] == -dy and s[3] == flip
-            )
-            if flip:
-                src = zsend
-                dst = zbuf.at[opposite - 8]
-                here = zbuf.at[k - 8]
-            else:
-                src = face(field, ysend, dx, dy)
-                dst = halo(field, ybuf, -dx, -dy)
-                here = halo(field, ybuf, dx, dy)
-            target = {"gx": gx + dx, "gy": gy + dy, "col": 1 - col if flip else col}
-            out = pltpu.make_async_remote_copy(
-                src_ref=src, dst_ref=dst, send_sem=halo_send.at[phase, k],
-                recv_sem=halo_recv.at[phase, opposite], device_id=target, device_id_type=MESH_ID,
-            )
-            arrive = pltpu.make_async_remote_copy(
-                src_ref=here, dst_ref=here, send_sem=halo_send.at[phase, k],
-                recv_sem=halo_recv.at[phase, k], device_id=target, device_id_type=MESH_ID,
-            )
-            result.append((cond, out, arrive))
-        return result
-
-    def guarded(cond, action):
-        if cond is None:
-            action()
-        else:
-            pl.when(cond)(action)
-
-    def zero_absent(field, ybuf, zbuf):
-        for k, (cond, dx, dy, flip) in enumerate(sources):
-            if cond is None:
-                continue
-
-            def clear(k=k, dx=dx, dy=dy, flip=flip):
-                if flip:
-                    zbuf[k - 8] = jnp.zeros(zbuf.shape[1:], f32)
-                else:
-                    part = halo(field, ybuf, dx, dy)
-                    part[...] = jnp.zeros(part.shape, f32)
-
-            pl.when(jnp.logical_not(cond))(clear)
-
-    def sum_copies(phase, msg, slots):
-        for other in peers:
-            pltpu.make_async_remote_copy(
-                src_ref=msg, dst_ref=slots.at[me], send_sem=sum_send.at[phase],
-                recv_sem=sum_recv.at[phase], device_id=other, device_id_type=MESH_ID,
-            ).start()
-        slots[me] = msg[...]
-        rest = slots.at[pl.ds(0, group - 1)]
-        return pltpu.make_async_remote_copy(
-            src_ref=rest, dst_ref=rest, send_sem=sum_send.at[phase],
-            recv_sem=sum_recv.at[phase], device_id=peers[0], device_id_type=MESH_ID,
-        )
-
-    zero_absent(f0, ybuf0, zbuf0)
-    zero_absent(f1, ybuf1, zbuf1)
-
-    pl.semaphore_wait(barrier, group - 1)
-
-    pending = []
-
-    def start(copies):
-        for cond, out, _ in copies:
-            guarded(cond, out.start)
-        pending.extend(copies)
-
-    def land(copies):
-        for cond, _, arrive in copies:
-            guarded(cond, arrive.wait_recv)
-
-    halo0 = exchange(0, f0, ysend0, ybuf0, zsend0, zbuf0)
-    start(halo0)
-    total0 = sum_copies(0, msg0, sums0)
-
     load_density.wait()
 
     def prepare(x, carry):
@@ -267,12 +276,12 @@
 
     def z_terms(zbuf):
         sign = jnp.where(col == 0, 0.25, -0.25)
-        h = zbuf[0]
-        ahead = jnp.where(xs == cx - 1, pltpu.roll(zbuf[2], cx - 1, 1), pltpu.roll(h, cz - 1, 1))
-        behind = jnp.where(xs == 0, pltpu.roll(zbuf[1], cz - cx + 1, 1), pltpu.roll(h, 1, 1))
+        h, before, after, under, over = (zbuf[k].astype(f32) for k in range(5))
+        ahead = jnp.where(xs == cx - 1, pltpu.roll(after, cx - 1, 1), pltpu.roll(h, cz - 1, 1))
+        behind = jnp.where(xs == 0, pltpu.roll(before, cz - cx + 1, 1), pltpu.roll(h, 1, 1))
         dxh = (ahead - behind) * sign
-        above = jnp.where(row == cy - 1, pltpu.roll(zbuf[4], cy - 1, 0), pltpu.roll(h, cy - 1, 0))
-        below = jnp.where(row == 0, pltpu.roll(zbuf[3], 1, 0), pltpu.roll(h, 1, 0))
+        above = jnp.where(row == cy - 1, pltpu.roll(over, cy - 1, 0), pltpu.roll(h, cy - 1, 0))
+        below = jnp.where(row == 0, pltpu.roll(under, 1, 0), pltpu.roll(h, 1, 0))
         dyh = (above - below) * sign
 
         def block(c):
@@ -349,7 +358,8 @@
                 s = source_s[part + c, x].astype(f32) + own[c]
                 part_s[part + c, x] = s + mu * (sx[c] + sy[c] + sz[c])
 
-    def y_terms(ybuf):
+    def y_terms(ybuf, yhalf):
+        ybuf[:, :, pl.ds(TOP, cx), :] = yhalf[...].astype(f32)
         for side, edge_rows, sign in ((0, pl.ds(0, 8), -0.25), (1, pl.ds(cy - 8, 8), 0.25)):
             mu = jnp.concatenate([mu_s[bx, edge_rows, :] for bx in range(cx // 8)], 0)
             lm = jnp.concatenate([lm_s[bx, edge_rows, :] for bx in range(cx // 8)], 0)
@@ -396,7 +406,10 @@
 
         lax.fori_loop(1, cx - 1, step, 0, unroll=2)
 
-    def outer(field):
+    def outer(field, xhalf):
+        field[:, 0] = xhalf[0].astype(f32)
+        field[:, cx + 1] = xhalf[1].astype(f32)
+
         def step(k, carry):
             stencil(field, k * (cx - 1))
             return carry
@@ -407,8 +420,8 @@
     load_source.wait()
     inner(f0)
     land(halo0)
-    outer(f0)
-    y_terms(ybuf0)
+    outer(f0, xhalf0)
+    y_terms(ybuf0, yhalf0)
     zk0 = z_terms(zbuf0)
     total0.wait_recv()
     zm0 = mean_terms(sums0)
@@ -428,8 +441,14 @@
     packed, accs = lax.fori_loop(
         0, cx, sweep_one, (jnp.zeros((cy, cz), f32), zero_acc), unroll=2
     )
-    zsend1[...] = packed
-    halo1 = exchange(1, f1, ysend1, ybuf1, zsend1, zbuf1)
+    zsend1[...] = packed.astype(jnp.bfloat16)
+    ysend_half1[...] = ysend1[...].astype(jnp.bfloat16)
+    xsend[0] = f1[:, 1].astype(jnp.bfloat16)
+    xsend[1] = f1[:, cx].astype(jnp.bfloat16)
+    halo1 = exchange(
+        1, (xsend.at[0], xsend.at[1]), xhalf1,
+        ysend1, ysend_half1, ybuf1, yhalf1, zsend1, zbuf1,
+    )
     start(halo1)
     msg1[...] = to_row(accs)
     total1 = sum_copies(1, msg1, sums1)
@@ -437,8 +456,8 @@
     inner(f1)
     load_forward.wait()
     land(halo1)
-    outer(f1)
-    y_terms(ybuf1)
+    outer(f1, xhalf1)
+    y_terms(ybuf1, yhalf1)
     zk1 = z_terms(zbuf1)
     total1.wait_recv()
     zm1 = mean_terms(sums1)
@@ -505,6 +524,7 @@
     tile = (cx, cy, cz)
     y_halo = pltpu.VMEM((2, 6, TOP + cx + 8, cz), f32)
     y_face = pltpu.VMEM((2, 6, cx, cz), f32)
+    half = pltpu.VMEM((2, 6, 16, cz), jnp.bfloat16)
     table = material_table.T
     warm, source, density, forward, iface_cells, material_map, table, impedance = (
         pltpu.with_memory_space_constraint(a, pltpu.HBM)
@@ -520,9 +540,10 @@
         out_specs=(vmem, vmem),
         scratch_shapes=[
             field, field,
-            pltpu.VMEM((5, cy, cz), f32), pltpu.VMEM((5, cy, cz), f32),
-            pltpu.VMEM((cy, cz), f32), pltpu.VMEM((cy, cz), f32),
+            pltpu.VMEM((5, cy, cz), jnp.bfloat16), pltpu.VMEM((5, cy, cz), jnp.bfloat16),
+            pltpu.VMEM((cy, cz), jnp.bfloat16), pltpu.VMEM((cy, cz), jnp.bfloat16),
             y_halo, y_halo, y_face, y_face,
+            half, half, half, half, half, half, half,
             pltpu.VMEM((group, 1, cz), f32), pltpu.VMEM((group, 1, cz), f32),
             pltpu.VMEM((group, 1, cz), f32),
             pltpu.VMEM((1, cz), f32), pltpu.VMEM((1, cz), f32), pltpu.VMEM((1, cz), f32),

time: 26 us -> 25.4 us (0.977)
  Pallas kernels: 23.1 us -> 22.4 us
    pallas_call x1, Pallas kernels: 23.1 us -> 22.4 us  [shards(): pl.pallas_call(functools.partial(kernel, n_gx, n_gy, n_col), out_shape=(j...]
where the time goes in v5:
time: 25.4 us; the launch traced here: 25.2 us
  Pallas kernels  22.4 us (88%)
  local copies, waits for them, and re-layouts  1.47 us (6%)
  between operations  1.29 us (5%)
    pallas_call x1, Pallas kernels, shards(): pl.pallas_call(functools.partial(kernel, n_gx, n_gy, n_col), out_shape=(j...  22.4 us
    unnamed x2, local copies, waits for them, and re-layouts  1.47 us

profile of v5, /device:TPU:0, one launch (start us, length us, event | category | flops | bytes accessed | tf_op | source)
XLA Modules:
  0.0 25.2 jit_solution(16474714034701054749)
XLA Ops:
  1.3 22.4 %adjoint_sweeps.1 = (f32[6,16,16,128]{3,2,1,0:T(8,128)S(1)}, f32[8,16]{1,0:T(8,128)S(1)}) custom-call(bf16[6,16,16,128]{3,2,1,0:T(8,128)(2,1)} %warm_hbm.1, bf16[6,16,16,128]{3,2,1,0:T(8,128)(2,1)} %source_hbm.1, bf16[16,16,128]{2,1,0:T(8,128)(2,1)} %density_hbm.1, bf16[6,16,16,128]{3,2,1,0:T(8,128)(2,1)} %forward_hbm.1, s32[1,256]{1,0:T(1,128)} %cells_ref.1, ...), custom_call_target="tpu_custom_call" | custom-call | tf_op jit(solution)/shard_map/adjoint_sweeps/pallas_call | solution.py:533
  23.7 0.9 %copy.14 = f32[6,16,16,128]{3,2,1,0:T(8,128)} copy(f32[6,16,16,128]{3,2,1,0:T(8,128)S(1)} %get-tuple-element.8) | data formatting | bytes 1572864
  24.6 0.6 %copy.15 = f32[16,8]{0,1:T(8,128)} copy(f32[16,8]{0,1:T(8,128)S(1)} %bitcast.2) | data formatting | bytes 1024

commit v6 on v5

--- a/solution.py
+++ b/solution.py
@@ -438,18 +438,23 @@
             packed = pack(packed, new[c], c, x)
         return packed, tuple(grown)
 
+    def sweep_one_ends(k, carry):
+        return sweep_one(k * (cx - 1), carry)
+
     packed, accs = lax.fori_loop(
-        0, cx, sweep_one, (jnp.zeros((cy, cz), f32), zero_acc), unroll=2
-    )
-    zsend1[...] = packed.astype(jnp.bfloat16)
-    ysend_half1[...] = ysend1[...].astype(jnp.bfloat16)
+        0, 2, sweep_one_ends, (jnp.zeros((cy, cz), f32), zero_acc), unroll=2
+    )
     xsend[0] = f1[:, 1].astype(jnp.bfloat16)
     xsend[1] = f1[:, cx].astype(jnp.bfloat16)
     halo1 = exchange(
         1, (xsend.at[0], xsend.at[1]), xhalf1,
         ysend1, ysend_half1, ybuf1, yhalf1, zsend1, zbuf1,
     )
-    start(halo1)
+    start(halo1[:2])
+    packed, accs = lax.fori_loop(1, cx - 1, sweep_one, (packed, accs), unroll=2)
+    zsend1[...] = packed.astype(jnp.bfloat16)
+    ysend_half1[...] = ysend1[...].astype(jnp.bfloat16)
+    start(halo1[2:])
     msg1[...] = to_row(accs)
     total1 = sum_copies(1, msg1, sums1)
 

time: 25.4 us -> 25 us (0.984)
  Pallas kernels: 22.4 us -> 22.1 us
    pallas_call x1, Pallas kernels: 22.4 us -> 22.1 us  [shards(): pl.pallas_call(functools.partial(kernel, n_gx, n_gy, n_col), out_shape=(j...]
where the time goes in v6:
time: 25 us; the launch traced here: 24.9 us
  Pallas kernels  22.1 us (88%)
  local copies, waits for them, and re-layouts  1.47 us (6%)
  between operations  1.29 us (5%)
    pallas_call x1, Pallas kernels, shards(): pl.pallas_call(functools.partial(kernel, n_gx, n_gy, n_col), out_shape=(j...  22.1 us
    unnamed x2, local copies, waits for them, and re-layouts  1.47 us

profile of v6, /device:TPU:0, one launch (start us, length us, event | category | flops | bytes accessed | tf_op | source)
XLA Modules:
  0.0 24.9 jit_solution(14294355743493737571)
XLA Ops:
  1.3 22.1 %adjoint_sweeps.1 = (f32[6,16,16,128]{3,2,1,0:T(8,128)S(1)}, f32[8,16]{1,0:T(8,128)S(1)}) custom-call(bf16[6,16,16,128]{3,2,1,0:T(8,128)(2,1)} %warm_hbm.1, bf16[6,16,16,128]{3,2,1,0:T(8,128)(2,1)} %source_hbm.1, bf16[16,16,128]{2,1,0:T(8,128)(2,1)} %density_hbm.1, bf16[6,16,16,128]{3,2,1,0:T(8,128)(2,1)} %forward_hbm.1, s32[1,256]{1,0:T(1,128)} %cells_ref.1, ...), custom_call_target="tpu_custom_call" | custom-call | tf_op jit(solution)/shard_map/adjoint_sweeps/pallas_call | solution.py:538
  23.4 0.9 %copy.14 = f32[6,16,16,128]{3,2,1,0:T(8,128)} copy(f32[6,16,16,128]{3,2,1,0:T(8,128)S(1)} %get-tuple-element.8) | data formatting | bytes 1572864
  24.3 0.6 %copy.15 = f32[16,8]{0,1:T(8,128)} copy(f32[16,8]{0,1:T(8,128)S(1)} %bitcast.2) | data formatting | bytes 1024

commit v7 on v6

--- a/solution.py
+++ b/solution.py
@@ -324,7 +324,7 @@
                 slope_s[part // 3, px] = y_up(uy) - y_down(uy) + (shift_up(uz) - shift_down(uz))
             return carry
 
-        lax.fori_loop(0, 2, step, 0)
+        lax.fori_loop(0, 2, step, 0, unroll=2)
 
     def stencil(field, x):
         px = x + 1
@@ -414,13 +414,14 @@
             stencil(field, k * (cx - 1))
             return carry
 
-        lax.fori_loop(0, 2, step, 0)
+        lax.fori_loop(0, 2, step, 0, unroll=2)
         halo_slopes(field)
 
     load_source.wait()
     inner(f0)
-    land(halo0)
+    land(halo0[:2])
     outer(f0, xhalf0)
+    land(halo0[2:])
     y_terms(ybuf0, yhalf0)
     zk0 = z_terms(zbuf0)
     total0.wait_recv()
@@ -460,8 +461,9 @@
 
     inner(f1)
     load_forward.wait()
-    land(halo1)
+    land(halo1[:2])
     outer(f1, xhalf1)
+    land(halo1[2:])
     y_terms(ybuf1, yhalf1)
     zk1 = z_terms(zbuf1)
     total1.wait_recv()

time: 25 us -> 25 us (level)
  no operation moved by 1% of the time
where the time goes in v7:
time: 25 us; the launch traced here: 24.8 us
  Pallas kernels  22.1 us (88%)
  local copies, waits for them, and re-layouts  1.47 us (6%)
  between operations  1.29 us (5%)
    pallas_call x1, Pallas kernels, shards(): pl.pallas_call(functools.partial(kernel, n_gx, n_gy, n_col), out_shape=(j...  22.1 us
    unnamed x2, local copies, waits for them, and re-layouts  1.47 us

profile of v7, /device:TPU:0, one launch (start us, length us, event | category | flops | bytes accessed | tf_op | source)
XLA Modules:
  0.0 24.8 jit_solution(8815190620838665156)
XLA Ops:
  1.3 22.1 %adjoint_sweeps.1 = (f32[6,16,16,128]{3,2,1,0:T(8,128)S(1)}, f32[8,16]{1,0:T(8,128)S(1)}) custom-call(bf16[6,16,16,128]{3,2,1,0:T(8,128)(2,1)} %warm_hbm.1, bf16[6,16,16,128]{3,2,1,0:T(8,128)(2,1)} %source_hbm.1, bf16[16,16,128]{2,1,0:T(8,128)(2,1)} %density_hbm.1, bf16[6,16,16,128]{3,2,1,0:T(8,128)(2,1)} %forward_hbm.1, s32[1,256]{1,0:T(1,128)} %cells_ref.1, ...), custom_call_target="tpu_custom_call" | custom-call | tf_op jit(solution)/shard_map/adjoint_sweeps/pallas_call | solution.py:540
  23.4 0.9 %copy.14 = f32[6,16,16,128]{3,2,1,0:T(8,128)} copy(f32[6,16,16,128]{3,2,1,0:T(8,128)S(1)} %get-tuple-element.8) | data formatting | bytes 1572864
  24.3 0.6 %copy.15 = f32[16,8]{0,1:T(8,128)} copy(f32[16,8]{0,1:T(8,128)S(1)} %bitcast.2) | data formatting | bytes 1024
